TPU v7x, 256 devices: a whole 4x4x8 slice. The times are simulated.
256 devices in a mesh: ctx: 32 (over x, z_lo, core), tp: 8 (over y, z_hi).
Axes of the slice: x: 4, y: 4, z: 8 (z_hi: 2, z_lo: 4; z = z_hi * 4 + z_lo), core: 2. Of those that a mesh axis runs over, the one named last changes fastest.
Arguments:
- query: bfloat16 [16384, 3072], P('ctx', 'tp'), may hold values from -32 to 32
- keys: bfloat16 [16384, 3072], P('ctx', 'tp'), may hold values from -12 to 12
- values: bfloat16 [16384, 3072], P('ctx', 'tp'), may hold values from -6 to 6
- image_ids: int32 [16384], P('ctx'), may hold values from 0 to 31, never falling along the last dimension, each value on 1 to 1024 neighbouring positions
- out_weight: bfloat16 [3072, 3072], P('tp'), may hold values from -0.109375 to 0.109375
- cotangent: bfloat16 [16384, 3072], P('ctx', 'tp'), may hold values from -6 to 6
Outputs:
- mixed: bfloat16 [16384, 3072], P('ctx', 'tp')
- grad_query: bfloat16 [16384, 3072], P('ctx', 'tp')
- grad_keys: bfloat16 [16384, 3072], P('ctx', 'tp')
- grad_values: bfloat16 [16384, 3072], P('ctx', 'tp')
- grad_weight: bfloat16 [3072, 3072], P('tp')
Inputs may be any that keep to these rules, and one draw needn't show every extreme that they name: `image_ids`: never falls along the tokens; each image holds 1 to 1024 consecutive tokens and some image exactly 1024.
All inputs are finite; a program needn't handle non-finite values.
Results may differ from a plain program's by a relative error of at most 0.012.
Values may be sent and summed in bfloat16 or wider, within the bound.
A program may use at most 128 MiB of HBM per device.

v0:
```python
import jax
import jax.numpy as jnp
from jax import lax
from jax.sharding import PartitionSpec as P

HEAD_DIM = 128
REACH = 2


NEG = -1e30


def from_behind(x, axis, by):
    size = lax.axis_size(axis)
    pairs = [(i, i + by) for i in range(size) if 0 <= i + by < size]
    return lax.ppermute(x, axis, pairs)


def split_heads(x):
    return x.reshape(x.shape[0], -1, HEAD_DIM)


def on_device(query, keys, values, image_ids, out_weight, cotangent):
    rows = query.shape[0]
    scale = HEAD_DIM ** (-0.5)
    place = lax.axis_index("ctx")
    count = lax.axis_size("ctx")
    offsets = [step for step in range(-REACH, REACH + 1) if step != 0]
    near_info = {}
    for step in offsets:
        got_ids = from_behind(image_ids, "ctx", step)
        source = place - step
        valid = (source >= 0) & (source < count)
        ids = jnp.where(valid, got_ids, -1)
        meets = valid & (ids[rows - 1] >= image_ids[0]) & (ids[0] <= image_ids[rows - 1])
        near_info[step] = (ids, meets)
    q_three = split_heads(query)
    k_three = split_heads(keys)
    v_three = split_heads(values)
    heads_dev = q_three.shape[1]
    always = jnp.array(True)
    key_pieces = [(k_three, v_three, image_ids, always)]
    for step in offsets:
        near_k, near_v = from_behind((keys, values), "ctx", step)
        ids, meets = near_info[step]
        key_pieces.append((split_heads(near_k), split_heads(near_v), ids, meets))
    top = jnp.full((heads_dev, rows), NEG, jnp.float32)
    total = jnp.zeros((heads_dev, rows), jnp.float32)
    stored = []
    for k_piece, v_piece, ids, meets in key_pieces:
        mask = (image_ids[:, None] == ids[None, :])[None]

        def visit(state):
            old_top, old_total = state
            scores = (
                jnp.einsum("qhe,khe->hqk", q_three, k_piece, preferred_element_type=jnp.float32)
                * scale
            )
            scores = jnp.where(mask, scores, NEG)
            new_top = jnp.maximum(old_top, jnp.max(scores, axis=2))
            terms = jnp.where(mask, jnp.exp(scores - new_top[:, :, None]), 0.0)
            new_total = old_total * jnp.exp(old_top - new_top) + jnp.sum(terms, axis=2)
            return (scores, new_top, new_total)

        def pass_by(state):
            return (jnp.full((heads_dev, rows, rows), NEG, jnp.float32), state[0], state[1])

        scores, top, total = lax.cond(meets, visit, pass_by, (top, total))
        stored.append(scores)
    lse = top + jnp.log(total)
    accum = jnp.zeros((rows, heads_dev, HEAD_DIM), jnp.float32)
    for (k_piece, v_piece, ids, meets), scores in zip(key_pieces, stored):

        def add_values(acc):
            probs = jnp.exp(scores - lse[:, :, None]).astype(jnp.bfloat16)
            return acc + jnp.einsum(
                "hqk,khe->qhe", probs, v_piece, preferred_element_type=jnp.float32
            )

        accum = lax.cond(meets, add_values, lambda acc: acc, accum)
    attended = accum.reshape(rows, -1).astype(jnp.bfloat16)
    partial_out = jnp.dot(attended, out_weight, preferred_element_type=jnp.float32)
    mixed = lax.psum_scatter(partial_out, "tp", scatter_dimension=1, tiled=True).astype(
        jnp.bfloat16
    )
    full_cot = lax.all_gather(cotangent, "tp", axis=1, tiled=True)
    d_attended = lax.dot_general(
        full_cot, out_weight, (((1,), (1,)), ((), ())), preferred_element_type=jnp.float32
    ).astype(jnp.bfloat16)
    weight_part = lax.dot_general(
        attended, full_cot, (((0,), (0,)), ((), ())), preferred_element_type=jnp.float32
    )
    grad_weight = lax.psum(weight_part, "ctx").astype(jnp.bfloat16)
    g_three = split_heads(d_attended)
    delta = jnp.einsum(
        "qhe,qhe->hq", g_three.astype(jnp.float32), split_heads(attended).astype(jnp.float32)
    )
    query_acc = jnp.zeros((rows, heads_dev, HEAD_DIM), jnp.float32)
    for (k_piece, v_piece, ids, meets), scores in zip(key_pieces, stored):

        def add_query_grad(acc):
            weight = jnp.exp(scores - lse[:, :, None])
            dots = jnp.einsum("qhe,khe->hqk", g_three, v_piece, preferred_element_type=jnp.float32)
            dscores = (weight * (dots - delta[:, :, None])).astype(jnp.bfloat16)
            return acc + jnp.einsum(
                "hqk,khe->qhe", dscores, k_piece, preferred_element_type=jnp.float32
            )

        query_acc = lax.cond(meets, add_query_grad, lambda acc: acc, query_acc)
    grad_query = (query_acc * scale).reshape(rows, -1).astype(jnp.bfloat16)
    query_pieces = [(q_three, g_three, image_ids, lse, delta, always)]
    for step in offsets:
        near_q, near_g = from_behind((query, d_attended), "ctx", step)
        near_lse, near_delta = from_behind((lse, delta), "ctx", step)
        ids, meets = near_info[step]
        query_pieces.append(
            (split_heads(near_q), split_heads(near_g), ids, near_lse, near_delta, meets)
        )
    key_acc = jnp.zeros((rows, heads_dev, HEAD_DIM), jnp.float32)
    value_acc = jnp.zeros((rows, heads_dev, HEAD_DIM), jnp.float32)
    for q_piece, g_piece, ids, lse_piece, delta_piece, meets in query_pieces:

        def add_key_grads(state):
            k_acc, v_acc = state
            mask = (ids[:, None] == image_ids[None, :])[None]
            scores = (
                jnp.einsum("qhe,khe->hqk", q_piece, k_three, preferred_element_type=jnp.float32)
                * scale
            )
            weight = jnp.where(mask, jnp.exp(scores - lse_piece[:, :, None]), 0.0)
            v_acc = v_acc + jnp.einsum(
                "hqk,qhe->khe",
                weight.astype(jnp.bfloat16),
                g_piece,
                preferred_element_type=jnp.float32,
            )
            dots = jnp.einsum("qhe,khe->hqk", g_piece, v_three, preferred_element_type=jnp.float32)
            dscores = (weight * (dots - delta_piece[:, :, None])).astype(jnp.bfloat16)
            k_acc = k_acc + jnp.einsum(
                "hqk,qhe->khe", dscores, q_piece, preferred_element_type=jnp.float32
            )
            return (k_acc, v_acc)

        key_acc, value_acc = lax.cond(
            meets, add_key_grads, lambda state: state, (key_acc, value_acc)
        )
    grad_keys = (key_acc * scale).reshape(rows, -1).astype(jnp.bfloat16)
    grad_values = value_acc.reshape(rows, -1).astype(jnp.bfloat16)
    return (mixed, grad_query, grad_keys, grad_values, grad_weight)


def solution(mesh):
    placed = (
        P("ctx", "tp"),
        P("ctx", "tp"),
        P("ctx", "tp"),
        P("ctx"),
        P("tp", None),
        P("ctx", "tp"),
    )
    return jax.shard_map(
        on_device,
        mesh=mesh,
        in_specs=placed,
        out_specs=(P("ctx", "tp"), P("ctx", "tp"), P("ctx", "tp"), P("ctx", "tp"), P("tp", None)),
        check_vma=False,
    )
```

profile of v0, /device:TPU:199, one launch (start us, length us, event | category | flops | bytes accessed | tf_op | source)
XLA Modules:
  0.0 502.8 jit_solution(16748405955379395885)
XLA Ops:
  30.6 6.2 %collective-permute-start.5 = (bf16[512,384]{0,1:T(8,128)(2,1)S(1)}, bf16[512,384]{0,1:T(8,128)(2,1)}, u32[]{:S(2)}, u32[]{:S(2)}) collective-permute-start(bf16[512,384]{0,1:T(8,128)(2,1)S(1)} %copy.63), channel_id=1, source_target_pairs={{8,0},{16,8},{24,16},{32,24},{40,32},{48,40},{56,48},{64,56},{72,6... | collective-permute-start | bytes 1179656 | tf_op jit(solution)/shard_map/ppermute | solution.py:16
  50.0 3.4 collective-permute-start.8
  60.8 6.9 %conditional.16 = (f32[3,512,512]{1,2,0:T(8,128)}, f32[3,512]{1,0:T(4,128)S(1)}, f32[3,512]{1,0:T(4,128)S(1)}) conditional(s32[]{:T(128)} %convert_element_type.151, (f32[3,512]{1,0:T(4,128)S(1)}, f32[3,512]{1,0:T(4,128)S(1)}) %tuple.141, (s32[512]{0:T(512)S(1)}, s32[512]{0:T(512)}, bf16[512,3,128]{0,2,1:T(8,128)(2,1)S(1)}, ...), branch_computations={%region_2.3_spmd, %region_3.6_spmd} | conditional | flops 206310400 | bytes 7948312 | solution.py:68
  61.7 3.4 fusion.147
  69.6 6.2 %conditional.17 = (f32[3,512,512]{1,2,0:T(8,128)}, f32[3,512]{1,0:T(4,128)S(1)}, f32[3,512]{1,0:T(4,128)S(1)}) conditional(s32[]{:T(128)} %convert_element_type.150, (f32[3,512]{1,0:T(4,128)S(1)}, f32[3,512]{1,0:T(4,128)S(1)}) %tuple.143, (s32[512]{0:T(512)S(1)}, s32[512]{0:T(512)S(1)}, bf16[512,3,128]{0,2,1:T(8,128)(2,1)S(1)}, ...), branch_computations={%region_6.7_spmd, %region_7.10_spmd} | conditional | flops 206310400 | bytes 7948312 | solution.py:68
  69.9 3.4 fusion.148
  77.8 6.3 %conditional.18 = (f32[3,512,512]{1,2,0:T(8,128)}, f32[3,512]{1,0:T(4,128)S(1)}, f32[3,512]{1,0:T(4,128)S(1)}) conditional(s32[]{:T(128)} %convert_element_type.149, (f32[3,512]{1,0:T(4,128)S(1)}, f32[3,512]{1,0:T(4,128)S(1)}) %tuple.145, (s32[512]{0:T(512)S(1)}, s32[512]{0:T(512)S(1)}, bf16[512,3,128]{0,2,1:T(8,128)(2,1)S(1)}, ...), branch_computations={%region_10.11_spmd, %region_11.14_spmd} | conditional | flops 206310400 | bytes 7948312 | solution.py:68
  78.0 3.6 fusion.149
  84.1 6.5 %conditional.19 = (f32[3,512,512]{1,2,0:T(8,128)}, f32[3,512]{1,0:T(4,128)S(1)}, f32[3,512]{1,0:T(4,128)S(1)}) conditional(s32[]{:T(128)} %convert_element_type.148, (f32[3,512]{1,0:T(4,128)S(1)}, f32[3,512]{1,0:T(4,128)S(1)}) %tuple.147, (s32[512]{0:T(512)S(1)}, s32[512]{0:T(512)S(1)}, bf16[512,3,128]{0,2,1:T(8,128)(2,1)S(1)}, ...), branch_computations={%region_14.15_spmd, %region_15.18_spmd} | conditional | flops 206310400 | bytes 7948312 | solution.py:68
  84.4 3.5 fusion.150
  93.8 6.3 %conditional.20 = (f32[512,3,128]{2,0,1:T(8,128)S(1)}) conditional(s32[]{:T(128)} %convert_element_type.151, f32[512,3,128]{2,0,1:T(8,128)S(1)} %fusion.130, (f32[3,512]{1,0:T(4,128)S(1)}, f32[3,512,512]{1,2,0:T(8,128)}, bf16[512,3,128]{0,2,1:T(8,128)(2,1)}, f32[512,3,128]{2,0,1:T(8,128)S(1)}) %tuple.149), branch_computations={%region_18.19_spmd, %region_19.20_spmd} | conditional | flops 203096064 | bytes 11409416 | solution.py:80
  93.8 3.5 copy.82
  100.1 6.3 %conditional.21 = (f32[512,3,128]{2,0,1:T(8,128)S(1)}) conditional(s32[]{:T(128)} %convert_element_type.150, f32[512,3,128]{2,0,1:T(8,128)S(1)} %get-tuple-element.775, (f32[3,512]{1,0:T(4,128)S(1)}, f32[3,512,512]{1,2,0:T(8,128)}, bf16[512,3,128]{0,2,1:T(8,128)(2,1)}, f32[512,3,128]{2,0,1:T(8,128)S(1)}) %tuple.150), branch_computations={%region_20.21_spmd, %region_21.22_spmd} | conditional | flops 203096064 | bytes 11409416 | solution.py:80
  100.1 3.5 copy.85
  106.5 4.6 collective-permute-done.10
  111.1 6.3 %conditional.22 = (f32[512,3,128]{2,0,1:T(8,128)S(1)}) conditional(s32[]{:T(128)} %convert_element_type.149, f32[512,3,128]{2,0,1:T(8,128)S(1)} %get-tuple-element.776, (f32[3,512]{1,0:T(4,128)S(1)}, f32[3,512,512]{1,2,0:T(8,128)}, bf16[512,3,128]{0,2,1:T(8,128)(2,1)}, f32[512,3,128]{2,0,1:T(8,128)S(1)}) %tuple.151), branch_computations={%region_22.23_spmd, %region_23.24_spmd} | conditional | flops 203096064 | bytes 11409416 | solution.py:80
  111.1 3.5 copy.88
  120.2 6.3 %conditional.23 = (f32[512,3,128]{2,0,1:T(8,128)S(1)}) conditional(s32[]{:T(128)} %convert_element_type.148, f32[512,3,128]{2,0,1:T(8,128)S(1)} %get-tuple-element.777, (f32[3,512]{1,0:T(4,128)S(1)}, f32[3,512,512]{1,2,0:T(8,128)}, bf16[512,3,128]{0,2,1:T(8,128)(2,1)}, f32[512,3,128]{2,0,1:T(8,128)S(1)}) %tuple.152), branch_computations={%region_24.25_spmd, %region_25.26_spmd} | conditional | flops 203096064 | bytes 11409416 | solution.py:80
  120.2 3.5 copy.91
  127.4 5.5 %fusion.160 = f32[512,3072]{1,0:T(8,128)} fusion(bf16[512,384]{0,1:T(8,128)(2,1)} %bitcast.185, bf16[384,3072]{1,0:T(8,128)(2,1)S(1)} %copy-done), kind=kOutput, calls=%fused_computation.186 | convolution fusion | flops 1207959552 | bytes 9043968 | tf_op jit(solution)/shard_map/dot_general | solution.py:82
  145.3 5.6 %fusion.162 = f32[384,3072]{1,0:T(8,128)} fusion(bf16[512,384]{0,1:T(8,128)(2,1)S(1)} %bitcast.186, bf16[512,3072]{1,0:T(8,128)(2,1)} %all-gather.2.cloned.1.call-done), kind=kOutput, calls=%fused_computation.188 | convolution fusion | flops 1207959552 | bytes 8257536 | tf_op jit(solution)/shard_map/dot_general | solution.py:90
  153.2 215.3 %all-reduce.1 = bf16[384,3072]{1,0:T(8,128)(2,1)} all-reduce(f32[384,3072]{1,0:T(8,128)} %fusion.162), channel_id=1, replica_groups=mesh['ctx'=32,'tp'=8] {'ctx'}, use_global_device_ids=true, to_apply=%region_43.44 | all-reduce | flops 1179648 | bytes 7077888 | tf_op jit(solution)/shard_map/psum | solution.py:93
  371.6 5.4 %collective-permute-start.21 = (f32[3,512]{1,0:T(4,128)S(1)}, f32[3,512]{1,0:T(4,128)S(1)}, u32[]{:S(2)}, u32[]{:S(2)}) collective-permute-start(f32[3,512]{1,0:T(4,128)S(1)} %log_add_fusion), channel_id=1, source_target_pairs={{0,8},{8,16},{16,24},{24,32},{32,40},{40,48},{48,56},{56,64},{64,7... | collective-permute-start | bytes 18440 | tf_op jit(solution)/shard_map/ppermute | solution.py:16
  382.9 4.6 collective-permute-start.18
  387.5 5.8 %collective-permute-start.19 = (f32[3,512]{1,0:T(4,128)S(1)}, f32[3,512]{1,0:T(4,128)S(1)}, u32[]{:S(2)}, u32[]{:S(2)}) collective-permute-start(f32[3,512]{1,0:T(4,128)S(1)} %fusion.138), channel_id=1, source_target_pairs={{8,0},{16,8},{24,16},{32,24},{40,32},{48,40},{56,48},{64,56},{72,6... | collective-permute-start | bytes 18440 | tf_op jit(solution)/shard_map/ppermute | solution.py:16
  404.5 7.2 %conditional.24 = (f32[512,3,128]{2,0,1:T(8,128)S(1)}) conditional(s32[]{:T(128)} %convert_element_type.151, f32[512,3,128]{2,0,1:T(8,128)S(1)} %fusion.134, (f32[3,512]{1,0:T(4,128)S(1)}, f32[3,512,512]{1,2,0:T(8,128)}, bf16[512,3,128]{0,2,1:T(8,128)(2,1)}, bf16[512,3,128]{0,2,1:T(8,128)(2,1)}, f32[3,512]{1,0:T(4,128)S(1)}, ...), branch_computations={%region_27.28_spmd, %region_28.29_spmd} | conditional | flops 405995520 | bytes 12201992 | solution.py:109
  404.6 3.6 copy.99
  408.2 3.5 fusion.18
  411.7 7.2 %conditional.25 = (f32[512,3,128]{2,0,1:T(8,128)S(1)}) conditional(s32[]{:T(128)} %convert_element_type.150, f32[512,3,128]{2,0,1:T(8,128)S(1)} %get-tuple-element.779, (f32[3,512]{1,0:T(4,128)S(1)}, f32[3,512,512]{1,2,0:T(8,128)}, bf16[512,3,128]{0,2,1:T(8,128)(2,1)}, bf16[512,3,128]{0,2,1:T(8,128)(2,1)}, f32[3,512]{1,0:T(4,128)S(1)}, ...), branch_computations={%region_29.30_spmd, %region_30.31_spmd} | conditional | flops 405995520 | bytes 12201992 | solution.py:109
  411.7 3.6 copy.103
  415.4 3.5 fusion.21
  418.9 7.2 %conditional.26 = (f32[512,3,128]{2,0,1:T(8,128)S(1)}) conditional(s32[]{:T(128)} %convert_element_type.149, f32[512,3,128]{2,0,1:T(8,128)S(1)} %get-tuple-element.780, (f32[3,512]{1,0:T(4,128)S(1)}, f32[3,512,512]{1,2,0:T(8,128)}, bf16[512,3,128]{0,2,1:T(8,128)(2,1)}, bf16[512,3,128]{0,2,1:T(8,128)(2,1)}, f32[3,512]{1,0:T(4,128)S(1)}, ...), branch_computations={%region_31.32_spmd, %region_32.33_spmd} | conditional | flops 405995520 | bytes 12201992 | solution.py:109
  418.9 3.6 copy.107
  422.5 3.5 fusion.24
  426.1 9.3 %conditional.27 = (f32[512,3,128]{0,2,1:T(8,128)S(1)}) conditional(s32[]{:T(128)} %convert_element_type.148, f32[512,3,128]{2,0,1:T(8,128)S(1)} %get-tuple-element.781, (f32[3,512]{1,0:T(4,128)S(1)}, f32[3,512,512]{1,2,0:T(8,128)}, bf16[512,3,128]{0,2,1:T(8,128)(2,1)}, bf16[512,3,128]{0,2,1:T(8,128)(2,1)}, f32[3,512]{1,0:T(4,128)S(1)}, ...), branch_computations={%region_33.34_spmd, %region_34.35_spmd} | conditional | flops 405995520 | bytes 13774856 | solution.py:109
  426.1 3.6 copy.111
  429.7 4.3 fusion.27
  440.3 13.4 %conditional.28 = (f32[512,3,128]{2,0,1:T(8,128)}, f32[512,3,128]{2,0,1:T(8,128)S(1)}) conditional(s32[]{:T(128)} %convert_element_type.151, (f32[512,3,128]{2,0,1:T(8,128)}, f32[512,3,128]{0,2,1:T(8,128)S(1)}) %tuple.157, (s32[512]{0:T(512)}, s32[512]{0:T(512)}, bf16[512,3,128]{0,2,1:T(8,128)(2,1)}, bf16[512,3,128]{0,2,1:T(8,128)(2,1)S(1)}, ...), branch_computations={%region_35.36_spmd, %region_36.37_spmd} | conditional | flops 813826048 | bytes 17381476 | solution.py:144
  445.0 5.1 %fusion.43 = f32[512,3,128]{2,0,1:T(8,128)} fusion(f32[512,3,128]{2,0,1:T(8,128)} %get-tuple-element.408, bf16[512,3,128]{0,2,1:T(8,128)(2,1)} %get-tuple-element.661, f32[3,512,512]{2,1,0:T(8,128)} %fusion.156, bf16[512,3,128]{0,2,1:T(8,128)(2,1)} %get-tuple-element.664, bf16[512,3,128]{0,2,1:T(8,128)(2,1)} %get-tuple-element.665, ...), kind=kOutput, calls=%fused_computation.64 | convolution fusion | flops 407568384 | bytes 6172672 | tf_op jit(solution)/shard_map/cond/branch_1_fun/hqk,qhe->khe/dot_general | solution.py:139
  450.4 3.4 fusion.40
  453.8 12.1 %conditional.29 = ((f32[512,3,128]{2,0,1:T(8,128)}, f32[512,3,128]{2,0,1:T(8,128)S(1)})) conditional(s32[]{:T(128)} %convert_element_type.150, (f32[512,3,128]{2,0,1:T(8,128)}, f32[512,3,128]{2,0,1:T(8,128)S(1)}) %conditional.28, (s32[512]{0:T(512)S(1)}, s32[512]{0:T(512)}, bf16[512,3,128]{0,2,1:T(8,128)(2,1)}, ...), branch_computations={%region_37.38_spmd, %region_38.39_spmd} | conditional | flops 813826048 | bytes 15759412 | solution.py:144
  457.4 5.1 %fusion.63 = f32[512,3,128]{2,0,1:T(8,128)} fusion(f32[512,3,128]{2,0,1:T(8,128)} %get-tuple-element.418, bf16[512,3,128]{0,2,1:T(8,128)(2,1)} %get-tuple-element.671, f32[3,512,512]{2,1,0:T(8,128)} %fusion.157, bf16[512,3,128]{0,2,1:T(8,128)(2,1)} %get-tuple-element.674, bf16[512,3,128]{0,2,1:T(8,128)(2,1)} %get-tuple-element.675, ...), kind=kOutput, calls=%fused_computation.82 | convolution fusion | flops 407568384 | bytes 6172672 | tf_op jit(solution)/shard_map/cond/branch_1_fun/hqk,qhe->khe/dot_general | solution.py:139
  462.6 3.4 fusion.60
  466.0 12.4 %conditional.30 = (f32[512,3,128]{2,0,1:T(8,128)}, f32[512,3,128]{2,0,1:T(8,128)S(1)}, bf16[512,3,128]{0,2,1:T(8,128)(2,1)S(1)}) conditional(s32[]{:T(128)} %convert_element_type.149, (f32[512,3,128]{2,0,1:T(8,128)}, f32[512,3,128]{2,0,1:T(8,128)S(1)}) %get-tuple-element.782, (s32[512]{0:T(512)S(1)}, s32[512]{0:T(512)}, ...), branch_computations={%region_39.40_spmd, %region_40.41_spmd} | conditional | flops 813826048 | bytes 16939060 | solution.py:144
  469.7 5.1 %fusion.83 = f32[512,3,128]{2,0,1:T(8,128)} fusion(f32[512,3,128]{2,0,1:T(8,128)} %get-tuple-element.428, bf16[512,3,128]{0,2,1:T(8,128)(2,1)} %get-tuple-element.681, f32[3,512,512]{2,1,0:T(8,128)} %fusion.158, bf16[512,3,128]{0,2,1:T(8,128)(2,1)} %get-tuple-element.684, bf16[512,3,128]{0,2,1:T(8,128)(2,1)} %get-tuple-element.685, ...), kind=kOutput, calls=%fused_computation.100 | convolution fusion | flops 407568384 | bytes 6172672 | tf_op jit(solution)/shard_map/cond/branch_1_fun/hqk,qhe->khe/dot_general | solution.py:139
  474.9 3.4 fusion.80
  478.5 12.8 %conditional.31 = (f32[512,3,128]{2,0,1:T(8,128)}, bf16[512,384]{1,0:T(8,128)(2,1)}) conditional(s32[]{:T(128)} %convert_element_type.148, (f32[512,3,128]{2,0,1:T(8,128)}, bf16[512,3,128]{0,2,1:T(8,128)(2,1)S(1)}) %tuple.196, (s32[512]{0:T(512)S(1)}, s32[512]{0:T(512)}, bf16[512,384]{0,1:T(8,128)(2,1)}, bf16[512,3,128]{0,2,1:T(8,128)(2,1)S(1)}, ...), branch_computations={%region_41.42_spmd, %region_42.43_spmd} | conditional | flops 814022656 | bytes 17725484 | solution.py:144
  482.1 5.2 %fusion.103 = f32[512,3,128]{2,0,1:T(8,128)} fusion(f32[512,3,128]{2,0,1:T(8,128)} %get-tuple-element.438, bf16[512,3,128]{0,2,1:T(8,128)(2,1)} %bitcast.17, f32[3,512,512]{2,1,0:T(8,128)} %fusion.159, bf16[512,3,128]{0,2,1:T(8,128)(2,1)} %bitcast.18, bf16[512,3,128]{0,2,1:T(8,128)(2,1)} %get-tuple-element.697, f32[3,512]{1,0:T(4,128)} %get-tuple-element.446, ...), kind=kOutput, calls=%fused_computation.118 | convolution fusion | flops 407568384 | bytes 6172672 | tf_op jit(solution)/shard_map/cond/branch_1_fun/hqk,qhe->khe/dot_general | solution.py:139
  (192 shorter events, 132.0 us)
Async XLA Ops:
  7.2 120.3 %copy-start = (bf16[384,3072]{1,0:T(8,128)(2,1)S(1)}, bf16[384,3072]{1,0:T(8,128)(2,1)}, u32[]{:S(2)}) copy-start(bf16[384,3072]{1,0:T(8,128)(2,1)} %param.42) | copy-start | bytes 7077892
  7.2 138.1 %all-gather.2.cloned.1.call-start = ((), (), s32[]{:S(2)}) async-start(), calls=%async_computation.2 | async-start | bytes 3538944 | tf_op jit(solution)/shard_map/all_gather | solution.py:86
  7.9 485.9 %reduce-scatter.2.cloned.1.call-start = ((), (), s32[]{:S(2)}) async-start(), calls=%async_computation.1 | async-start | bytes 7077888 | tf_op jit(solution)/shard_map/reduce_scatter | solution.py:83
  8.0 22.7 %collective-permute-start = (s32[512]{0:T(512)}, s32[512]{0:T(512)S(1)}, u32[]{:S(2)}, u32[]{:S(2)}) collective-permute-start(s32[512]{0:T(512)} %param.41), channel_id=1, source_target_pairs={{0,16},{8,24},{16,32},{24,40},{32,48},{40,56},{48,64},{56,72},{64,... | collective-permute-start | bytes 6152 | tf_op jit(solution)/shard_map/ppermute | solution.py:16
  10.6 26.9 %collective-permute-start.1 = (s32[512]{0:T(512)}, s32[512]{0:T(512)S(1)}, u32[]{:S(2)}, u32[]{:S(2)}) collective-permute-start(s32[512]{0:T(512)} %param.41), channel_id=1, source_target_pairs={{0,8},{8,16},{16,24},{24,32},{32,40},{40,48},{48,56},{56,64},{64,7... | collective-permute-start | bytes 6152 | tf_op jit(solution)/shard_map/ppermute | solution.py:16
  12.5 27.5 %collective-permute-start.2 = (s32[512]{0:T(512)}, s32[512]{0:T(512)S(1)}, u32[]{:S(2)}, u32[]{:S(2)}) collective-permute-start(s32[512]{0:T(512)} %param.41), channel_id=1, source_target_pairs={{8,0},{16,8},{24,16},{32,24},{40,32},{48,40},{56,48},{64,56},{72,6... | collective-permute-start | bytes 6152 | tf_op jit(solution)/shard_map/ppermute | solution.py:16
  15.4 34.6 %collective-permute-start.3 = (s32[512]{0:T(512)}, s32[512]{0:T(512)S(1)}, u32[]{:S(2)}, u32[]{:S(2)}) collective-permute-start(s32[512]{0:T(512)} %param.41), channel_id=1, source_target_pairs={{16,0},{24,8},{32,16},{40,24},{48,32},{56,40},{64,48},{72,56},{80,... | collective-permute-start | bytes 6152 | tf_op jit(solution)/shard_map/ppermute | solution.py:16
  19.9 20.2 %copy-start.4 = (bf16[512,384]{0,1:T(8,128)(2,1)}, bf16[512,384]{0,1:T(8,128)(2,1)S(1)}, u32[]{:S(2)}) copy-start(bf16[512,384]{0,1:T(8,128)(2,1)S(1)} %copy.63) | copy-start | bytes 1179652
  19.9 37.9 %collective-permute-start.4 = (bf16[512,384]{0,1:T(8,128)(2,1)S(1)}, bf16[512,384]{0,1:T(8,128)(2,1)}, u32[]{:S(2)}, u32[]{:S(2)}) collective-permute-start(bf16[512,384]{0,1:T(8,128)(2,1)S(1)} %copy.63), channel_id=1, source_target_pairs={{16,0},{24,8},{32,16},{40,24},{48,32},{56,40},{64,48},{72,56},{80,... | collective-permute-start | bytes 1179656 | tf_op jit(solution)/shard_map/ppermute | solution.py:16
  30.6 37.0 %collective-permute-start.5 = (bf16[512,384]{0,1:T(8,128)(2,1)S(1)}, bf16[512,384]{0,1:T(8,128)(2,1)}, u32[]{:S(2)}, u32[]{:S(2)}) collective-permute-start(bf16[512,384]{0,1:T(8,128)(2,1)S(1)} %copy.63), channel_id=1, source_target_pairs={{8,0},{16,8},{24,16},{32,24},{40,32},{48,40},{56,48},{64,56},{72,6... | collective-permute-start | bytes 1179656 | tf_op jit(solution)/shard_map/ppermute | solution.py:16
  36.9 47.2 %copy-start.15 = (s32[512]{0:T(512)}, s32[512]{0:T(512)S(1)}, u32[]{:S(2)}) copy-start(s32[512]{0:T(512)S(1)} %broadcast_select_fusion.3) | copy-start | bytes 6148
  37.5 38.3 %collective-permute-start.6 = (bf16[512,384]{0,1:T(8,128)(2,1)S(1)}, bf16[512,384]{0,1:T(8,128)(2,1)}, u32[]{:S(2)}, u32[]{:S(2)}) collective-permute-start(bf16[512,384]{0,1:T(8,128)(2,1)S(1)} %copy.63), channel_id=1, source_target_pairs={{0,8},{8,16},{16,24},{24,32},{32,40},{40,48},{48,56},{56,64},{64,7... | collective-permute-start | bytes 1179656 | tf_op jit(solution)/shard_map/ppermute | solution.py:16
  39.4 38.3 %copy-start.17 = (s32[512]{0:T(512)}, s32[512]{0:T(512)S(1)}, u32[]{:S(2)}) copy-start(s32[512]{0:T(512)S(1)} %broadcast_select_fusion.2) | copy-start | bytes 6148
  40.0 44.1 %collective-permute-start.7 = (bf16[512,384]{0,1:T(8,128)(2,1)S(1)}, bf16[512,384]{0,1:T(8,128)(2,1)}, u32[]{:S(2)}, u32[]{:S(2)}) collective-permute-start(bf16[512,384]{0,1:T(8,128)(2,1)S(1)} %copy.63), channel_id=1, source_target_pairs={{0,16},{8,24},{16,32},{24,40},{32,48},{40,56},{48,64},{56,72},{64,... | collective-permute-start | bytes 1179656 | tf_op jit(solution)/shard_map/ppermute | solution.py:16
  42.0 27.6 %copy-start.19 = (s32[512]{0:T(512)}, s32[512]{0:T(512)S(1)}, u32[]{:S(2)}) copy-start(s32[512]{0:T(512)S(1)} %broadcast_select_fusion.1) | copy-start | bytes 6148
  50.0 43.7 %collective-permute-start.8 = (bf16[512,384]{0,1:T(8,128)(2,1)}, bf16[512,384]{0,1:T(8,128)(2,1)}, u32[]{:S(2)}, u32[]{:S(2)}) collective-permute-start(bf16[512,384]{0,1:T(8,128)(2,1)} %copy.78), channel_id=1, source_target_pairs={{16,0},{24,8},{32,16},{40,24},{48,32},{56,40},{64,48},{72,56},{80,... | collective-permute-start | bytes 1179656 | tf_op jit(solution)/shard_map/ppermute | solution.py:16
  57.8 42.3 %collective-permute-start.9 = (bf16[512,384]{0,1:T(8,128)(2,1)}, bf16[512,384]{0,1:T(8,128)(2,1)}, u32[]{:S(2)}, u32[]{:S(2)}) collective-permute-start(bf16[512,384]{0,1:T(8,128)(2,1)} %copy.78), channel_id=1, source_target_pairs={{8,0},{16,8},{24,16},{32,24},{40,32},{48,40},{56,48},{64,56},{72,6... | collective-permute-start | bytes 1179656 | tf_op jit(solution)/shard_map/ppermute | solution.py:16
  67.7 43.4 %collective-permute-start.10 = (bf16[512,384]{0,1:T(8,128)(2,1)}, bf16[512,384]{0,1:T(8,128)(2,1)}, u32[]{:S(2)}, u32[]{:S(2)}) collective-permute-start(bf16[512,384]{0,1:T(8,128)(2,1)} %copy.78), channel_id=1, source_target_pairs={{0,8},{8,16},{16,24},{24,32},{32,40},{40,48},{48,56},{56,64},{64,7... | collective-permute-start | bytes 1179656 | tf_op jit(solution)/shard_map/ppermute | solution.py:16
  75.8 44.4 %collective-permute-start.11 = (bf16[512,384]{0,1:T(8,128)(2,1)}, bf16[512,384]{0,1:T(8,128)(2,1)}, u32[]{:S(2)}, u32[]{:S(2)}) collective-permute-start(bf16[512,384]{0,1:T(8,128)(2,1)} %copy.78), channel_id=1, source_target_pairs={{0,16},{8,24},{16,32},{24,40},{32,48},{40,56},{48,64},{56,72},{64,... | collective-permute-start | bytes 1179656 | tf_op jit(solution)/shard_map/ppermute | solution.py:16
  132.9 12.4 %copy-start.8 = (bf16[512,3,128]{0,2,1:T(8,128)(2,1)S(1)}, bf16[512,3,128]{0,2,1:T(8,128)(2,1)}, u32[]{:S(2)}) copy-start(bf16[512,3,128]{0,2,1:T(8,128)(2,1)} %copy.93) | copy-start | bytes 1179652
  132.9 238.7 %collective-permute-start.12 = (bf16[512,384]{0,1:T(8,128)(2,1)S(1)}, bf16[512,384]{0,1:T(8,128)(2,1)}, u32[]{:S(2)}, u32[]{:S(2)}) collective-permute-start(bf16[512,384]{0,1:T(8,128)(2,1)S(1)} %copy.62), channel_id=1, source_target_pairs={{16,0},{24,8},{32,16},{40,24},{48,32},{56,40},{64,48},{72,56},{80,... | collective-permute-start | bytes 1179656 | tf_op jit(solution)/shard_map/ppermute | solution.py:16
  135.0 244.1 %collective-permute-start.16 = (bf16[512,384]{0,1:T(8,128)(2,1)S(1)}, bf16[512,384]{0,1:T(8,128)(2,1)}, u32[]{:S(2)}, u32[]{:S(2)}) collective-permute-start(bf16[512,384]{0,1:T(8,128)(2,1)S(1)} %copy.62), channel_id=1, source_target_pairs={{8,0},{16,8},{24,16},{32,24},{40,32},{48,40},{56,48},{64,56},{72,6... | collective-permute-start | bytes 1179656 | tf_op jit(solution)/shard_map/ppermute | solution.py:16
  138.1 242.8 %collective-permute-start.20 = (bf16[512,384]{0,1:T(8,128)(2,1)S(1)}, bf16[512,384]{0,1:T(8,128)(2,1)}, u32[]{:S(2)}, u32[]{:S(2)}) collective-permute-start(bf16[512,384]{0,1:T(8,128)(2,1)S(1)} %copy.62), channel_id=1, source_target_pairs={{0,8},{8,16},{16,24},{24,32},{32,40},{40,48},{48,56},{56,64},{64,7... | collective-permute-start | bytes 1179656 | tf_op jit(solution)/shard_map/ppermute | solution.py:16
  140.6 242.4 %collective-permute-start.13 = (f32[3,512]{1,0:T(4,128)S(1)}, f32[3,512]{1,0:T(4,128)S(1)}, u32[]{:S(2)}, u32[]{:S(2)}) collective-permute-start(f32[3,512]{1,0:T(4,128)S(1)} %log_add_fusion), channel_id=1, source_target_pairs={{16,0},{24,8},{32,16},{40,24},{48,32},{56,40},{64,48},{72,56},{80,... | collective-permute-start | bytes 18440 | tf_op jit(solution)/shard_map/ppermute | solution.py:16
  143.3 244.2 %collective-permute-start.17 = (f32[3,512]{1,0:T(4,128)S(1)}, f32[3,512]{1,0:T(4,128)S(1)}, u32[]{:S(2)}, u32[]{:S(2)}) collective-permute-start(f32[3,512]{1,0:T(4,128)S(1)} %log_add_fusion), channel_id=1, source_target_pairs={{8,0},{16,8},{24,16},{32,24},{40,32},{48,40},{56,48},{64,56},{72,6... | collective-permute-start | bytes 18440 | tf_op jit(solution)/shard_map/ppermute | solution.py:16
  368.6 8.5 %copy-start.3 = (f32[3,512,512]{1,2,0:T(8,128)S(1)}, f32[3,512,512]{1,2,0:T(8,128)}, u32[]{:S(2)}) copy-start(f32[3,512,512]{1,2,0:T(8,128)} %copy-done.2) | copy-start | bytes 9437188
  368.6 8.5 %copy-start.7 = (pred[512,512]{0,1:T(8,128)(4,1)S(1)}, pred[512,512]{0,1:T(8,128)(4,1)}, u32[]{:S(2)}) copy-start(pred[512,512]{0,1:T(8,128)(4,1)} %copy-done.6) | copy-start | bytes 786436
  371.6 23.7 %copy-start.5 = (bf16[512,384]{0,1:T(8,128)(2,1)S(1)}, bf16[512,384]{0,1:T(8,128)(2,1)}, u32[]{:S(2)}) copy-start(bf16[512,384]{0,1:T(8,128)(2,1)} %copy-done.4) | copy-start | bytes 1179652
  371.6 21.7 %collective-permute-start.21 = (f32[3,512]{1,0:T(4,128)S(1)}, f32[3,512]{1,0:T(4,128)S(1)}, u32[]{:S(2)}, u32[]{:S(2)}) collective-permute-start(f32[3,512]{1,0:T(4,128)S(1)} %log_add_fusion), channel_id=1, source_target_pairs={{0,8},{8,16},{16,24},{24,32},{32,40},{40,48},{48,56},{56,64},{64,7... | collective-permute-start | bytes 18440 | tf_op jit(solution)/shard_map/ppermute | solution.py:16
  379.1 56.4 %collective-permute-start.14 = (bf16[512,384]{0,1:T(8,128)(2,1)}, bf16[512,384]{0,1:T(8,128)(2,1)}, u32[]{:S(2)}, u32[]{:S(2)}) collective-permute-start(bf16[512,384]{0,1:T(8,128)(2,1)} %convolution_convert_fusion), channel_id=1, source_target_pairs={{16,0},{24,8},{32,16},{40,24},{48,32},{56,40},{64,48},{72,56},{80,... | collective-permute-start | bytes 1179656 | tf_op jit(solution)/shard_map/ppermute | solution.py:16
  381.0 15.8 %collective-permute-start.15 = (f32[3,512]{1,0:T(4,128)S(1)}, f32[3,512]{1,0:T(4,128)S(1)}, u32[]{:S(2)}, u32[]{:S(2)}) collective-permute-start(f32[3,512]{1,0:T(4,128)S(1)} %fusion.138), channel_id=1, source_target_pairs={{16,0},{24,8},{32,16},{40,24},{48,32},{56,40},{64,48},{72,56},{80,... | collective-permute-start | bytes 18440 | tf_op jit(solution)/shard_map/ppermute | solution.py:16
  382.9 10.4 %copy-start.27 = (f32[3,512]{1,0:T(4,128)}, f32[3,512]{1,0:T(4,128)S(1)}, u32[]{:S(2)}) copy-start(f32[3,512]{1,0:T(4,128)S(1)} %collective-permute-done.13) | copy-start | bytes 18436
  382.9 54.4 %collective-permute-start.18 = (bf16[512,384]{0,1:T(8,128)(2,1)}, bf16[512,384]{0,1:T(8,128)(2,1)}, u32[]{:S(2)}, u32[]{:S(2)}) collective-permute-start(bf16[512,384]{0,1:T(8,128)(2,1)} %convolution_convert_fusion), channel_id=1, source_target_pairs={{8,0},{16,8},{24,16},{32,24},{40,32},{48,40},{56,48},{64,56},{72,6... | collective-permute-start | bytes 1179656 | tf_op jit(solution)/shard_map/ppermute | solution.py:16
  387.5 9.2 %copy-start.23 = (f32[3,512]{1,0:T(4,128)}, f32[3,512]{1,0:T(4,128)S(1)}, u32[]{:S(2)}) copy-start(f32[3,512]{1,0:T(4,128)S(1)} %collective-permute-done.17) | copy-start | bytes 18436
  387.5 11.2 %collective-permute-start.19 = (f32[3,512]{1,0:T(4,128)S(1)}, f32[3,512]{1,0:T(4,128)S(1)}, u32[]{:S(2)}, u32[]{:S(2)}) collective-permute-start(f32[3,512]{1,0:T(4,128)S(1)} %fusion.138), channel_id=1, source_target_pairs={{8,0},{16,8},{24,16},{32,24},{40,32},{48,40},{56,48},{64,56},{72,6... | collective-permute-start | bytes 18440 | tf_op jit(solution)/shard_map/ppermute | solution.py:16
  393.4 7.3 %collective-permute-start.23 = (f32[3,512]{1,0:T(4,128)S(1)}, f32[3,512]{1,0:T(4,128)S(1)}, u32[]{:S(2)}, u32[]{:S(2)}) collective-permute-start(f32[3,512]{1,0:T(4,128)S(1)} %fusion.138), channel_id=1, source_target_pairs={{0,8},{8,16},{16,24},{24,32},{32,40},{40,48},{48,56},{56,64},{64,7... | collective-permute-start | bytes 18440 | tf_op jit(solution)/shard_map/ppermute | solution.py:16
  396.8 81.6 %collective-permute-start.24 = (bf16[512,384]{0,1:T(8,128)(2,1)S(1)}, bf16[512,384]{0,1:T(8,128)(2,1)}, u32[]{:S(2)}, u32[]{:S(2)}) collective-permute-start(bf16[512,384]{0,1:T(8,128)(2,1)S(1)} %copy.62), channel_id=1, source_target_pairs={{0,16},{8,24},{16,32},{24,40},{32,48},{40,56},{48,64},{56,72},{64,... | collective-permute-start | bytes 1179656 | tf_op jit(solution)/shard_map/ppermute | solution.py:16
  398.7 67.2 %collective-permute-start.22 = (bf16[512,384]{0,1:T(8,128)(2,1)}, bf16[512,384]{0,1:T(8,128)(2,1)}, u32[]{:S(2)}, u32[]{:S(2)}) collective-permute-start(bf16[512,384]{0,1:T(8,128)(2,1)} %convolution_convert_fusion), channel_id=1, source_target_pairs={{0,8},{8,16},{16,24},{24,32},{32,40},{40,48},{48,56},{56,64},{64,7... | collective-permute-start | bytes 1179656 | tf_op jit(solution)/shard_map/ppermute | solution.py:16
  400.7 77.8 %collective-permute-start.26 = (bf16[512,384]{0,1:T(8,128)(2,1)}, bf16[512,384]{0,1:T(8,128)(2,1)}, u32[]{:S(2)}, u32[]{:S(2)}) collective-permute-start(bf16[512,384]{0,1:T(8,128)(2,1)} %convolution_convert_fusion), channel_id=1, source_target_pairs={{0,16},{8,24},{16,32},{24,40},{32,48},{40,56},{48,64},{56,72},{64,... | collective-permute-start | bytes 1179656 | tf_op jit(solution)/shard_map/ppermute | solution.py:16
  435.5 43.0 %collective-permute-start.25 = (f32[3,512]{1,0:T(4,128)S(1)}, f32[3,512]{1,0:T(4,128)}, u32[]{:S(2)}, u32[]{:S(2)}) collective-permute-start(f32[3,512]{1,0:T(4,128)S(1)} %log_add_fusion), channel_id=1, source_target_pairs={{0,16},{8,24},{16,32},{24,40},{32,48},{40,56},{48,64},{56,72},{64,... | collective-permute-start | bytes 18440 | tf_op jit(solution)/shard_map/ppermute | solution.py:16
  437.4 41.1 %collective-permute-start.27 = (f32[3,512]{1,0:T(4,128)S(1)}, f32[3,512]{1,0:T(4,128)}, u32[]{:S(2)}, u32[]{:S(2)}) collective-permute-start(f32[3,512]{1,0:T(4,128)S(1)} %fusion.138), channel_id=1, source_target_pairs={{0,16},{8,24},{16,32},{24,40},{32,48},{40,56},{48,64},{56,72},{64,... | collective-permute-start | bytes 18440 | tf_op jit(solution)/shard_map/ppermute | solution.py:16
  440.3 13.5 %copy-start.20 = (s32[512]{0:T(512)S(1)}, s32[512]{0:T(512)}, u32[]{:S(2)}) copy-start(s32[512]{0:T(512)} %copy-done.19) | copy-start | bytes 6148
  440.3 13.5 %copy-start.24 = (f32[3,512]{1,0:T(4,128)S(1)}, f32[3,512]{1,0:T(4,128)}, u32[]{:S(2)}) copy-start(f32[3,512]{1,0:T(4,128)} %copy-done.23) | copy-start | bytes 18436
  440.3 13.5 %copy-start.30 = (f32[3,512]{1,0:T(4,128)S(1)}, f32[3,512]{1,0:T(4,128)}, u32[]{:S(2)}) copy-start(f32[3,512]{1,0:T(4,128)} %copy-done.29) | copy-start | bytes 18436
  453.8 12.1 %copy-start.18 = (s32[512]{0:T(512)S(1)}, s32[512]{0:T(512)}, u32[]{:S(2)}) copy-start(s32[512]{0:T(512)} %copy-done.17) | copy-start | bytes 6148
  453.8 12.1 %copy-start.22 = (f32[3,512]{1,0:T(4,128)S(1)}, f32[3,512]{1,0:T(4,128)}, u32[]{:S(2)}) copy-start(f32[3,512]{1,0:T(4,128)} %copy-done.21) | copy-start | bytes 18436
  453.8 12.1 %copy-start.26 = (f32[3,512]{1,0:T(4,128)S(1)}, f32[3,512]{1,0:T(4,128)}, u32[]{:S(2)}) copy-start(f32[3,512]{1,0:T(4,128)} %copy-done.25) | copy-start | bytes 18436
  466.0 12.5 %copy-start.16 = (s32[512]{0:T(512)S(1)}, s32[512]{0:T(512)}, u32[]{:S(2)}) copy-start(s32[512]{0:T(512)} %copy-done.15) | copy-start | bytes 6148
  (15 other events, 61.1 us)
Sparse Core Ops, SparseCore 0:
  10.5 120.6 all-gather.1
  135.4 194.9 reduce-scatter.1
where the time goes:
time: 513 us; the launch traced here: 503 us
  blocking collectives  215 us (42%)
  matrix products  111 us (22%)
  starting transfers between devices  77.1 us (15%)
  local copies, waits for them, and re-layouts  45.6 us (9%)
  between operations  25.1 us (5%)
  other arithmetic  18.9 us (4%)
  waiting for transfers between devices  8.15 us (2%)
    psum x1, blocking collectives, on_device(): grad_weight = lax.psum(weight_part, 'ctx').astype(jnp.bfloat16)  215 us
    ppermute x28, starting transfers between devices, from_behind(): return lax.ppermute(x, axis, pairs)  77 us
    another operation x10, local copies, waits for them, and re-layouts  29 us
    dot_general x5, matrix products, add_key_grads(): jnp.einsum('hqk,qhe->khe', dscores, q_piece, preferred_element_type=jnp.f...  22.6 us
    dot_general x5, matrix products, add_query_grad(): jnp.einsum('hqk,khe->qhe', dscores, k_piece, preferred_element_type=jnp.f...  16.4 us
    dot_general x5, matrix products, add_key_grads(): jnp.einsum('hqk,qhe->khe', weight.astype(jnp.bfloat16), g_piece, preferre...  14.8 us
    dot_general x5, matrix products, visit(): jnp.einsum('qhe,khe->hqk', q_three, k_piece, preferred_element_type=jnp.f...  14.8 us
    dot_general x5, matrix products, add_values(): jnp.einsum('hqk,khe->qhe', probs, v_piece, preferred_element_type=jnp.flo...  14.4 us
  transfers between devices with their start and end apart: 30, of which 2 were waited for; matrix products, arithmetic and copies ran while one was open for 34% of the time, Pallas kernels for 0%

commit v1 on v0

v1 whole, which is shorter than its diff:
```python
import functools

import jax
import jax.numpy as jnp
from jax import lax
from jax.experimental import pallas as pl
from jax.experimental.pallas import tpu as pltpu
from jax.sharding import PartitionSpec as P

HEAD = 128
ROWS = 512
COLS = 384
HEADS_DEV = COLS // HEAD
TP = 8
FEATURES = TP * COLS
WINDOW = 5
OWN = 2
CHUNK = 256
KEY_CHUNKS = WINDOW * ROWS // CHUNK
PIECE_ROWS = 48
PIECE_COLS = 768
NEG = -1e30
SCALE = HEAD ** -0.5
EXP2_SCALE = SCALE * 1.4426950408889634
F32 = jnp.float32
BF16 = jnp.bfloat16
MESH = pl.DeviceIdType.MESH
VMEM = pl.BlockSpec(memory_space=pltpu.VMEM)
SMEM = pl.BlockSpec(memory_space=pltpu.SMEM)
LIMIT = 56 * 1024 * 1024


class Links:
    def __init__(self, send_sem, recv_sem):
        self.send_sem, self.recv_sem = send_sem, recv_sem
        self.sent = []

    def _copy(self, src, dst, role, where):
        return pltpu.make_async_remote_copy(
            src_ref=src,
            dst_ref=dst,
            send_sem=self.send_sem.at[role],
            recv_sem=self.recv_sem.at[role],
            device_id=where,
            device_id_type=MESH,
        )

    def send(self, src, dst, role, where):
        copy = self._copy(src, dst, role, where)
        copy.start()
        self.sent.append(copy)

    def arrive(self, dst, role, where):
        self._copy(dst, dst, role, where).wait_recv()

    def finish(self):
        for copy in self.sent:
            copy.wait_send()


def greet(peers):
    barrier = pltpu.get_barrier_semaphore()
    for where in peers:
        pl.semaphore_signal(barrier, inc=1, device_id=where, device_id_type=MESH)
    pl.semaphore_wait(barrier, len(peers))


def ctx_ring(place, step):
    return {"ctx": lax.rem(place + step + 32, 32)}


def columns(index):
    return pl.ds(pl.multiple_of(index * COLS, COLS), COLS)


def gather_kernel(
    ids_ref, k_ref, v_ref, cot_ref, w_ref,
    ids_all, k_all, v_all, cot_all, dat_ref,
    acc, send_sem, recv_sem,
):
    place = lax.axis_index("ctx")
    part = lax.axis_index("tp")
    core = lax.rem(place, 2)
    high = lax.rem(part, 2)
    after, before = ctx_ring(place, 2), ctx_ring(place, -2)
    sibling = {"ctx": place + 1 - 2 * core}
    up, down = lax.rem(part + 2, TP), lax.rem(part + 6, TP)
    over = part + 1 - 2 * high
    across = lax.rem(part + 4, TP)
    y_up, y_down, far = {"tp": up}, {"tp": down}, {"tp": over}
    greet([after, before, sibling, y_up, y_down, far])
    links = Links(send_sem, recv_sem)

    links.send(cot_ref, cot_all.at[part], 12, far)
    links.send(cot_ref, cot_all.at[part], 13, y_up)
    links.send(cot_ref, cot_all.at[part], 14, y_down)
    arrays = ((ids_ref, ids_all), (k_ref, k_all), (v_ref, v_all))
    for n, (own, window) in enumerate(arrays):
        links.send(own, window.at[0], 4 * n, after)
        links.send(own, window.at[4], 4 * n + 1, before)
        links.send(own, window.at[1 + 2 * core], 4 * n + 2, sibling)
    for own, window in arrays:
        window[OWN] = own[...]
    cot_all[part] = cot_ref[...]

    def project(block, first=False):
        term = lax.dot_general(
            cot_all[block],
            w_ref[:, columns(block)],
            (((1,), (1,)), ((), ())),
            preferred_element_type=F32,
        )
        if first:
            acc[...] = term
        else:
            acc[...] += term

    def relay(n):
        window = arrays[n][1]
        links.arrive(window.at[0], 4 * n, before)
        links.arrive(window.at[4], 4 * n + 1, after)
        links.send(
            window.at[4 * (1 - core)], window.at[3 - 2 * core], 4 * n + 3, sibling
        )

    def forward(low_block, high_block, low_role, high_role, role):
        links.arrive(cot_all.at[low_block], low_role, y_down)
        links.send(
            cot_all.at[low_block, pl.ds(0, ROWS // 2)],
            cot_all.at[low_block, pl.ds(0, ROWS // 2)],
            role,
            y_up,
        )
        links.arrive(cot_all.at[high_block], high_role, y_up)
        links.send(
            cot_all.at[high_block, pl.ds(ROWS // 2, ROWS // 2)],
            cot_all.at[high_block, pl.ds(ROWS // 2, ROWS // 2)],
            role + 1,
            y_down,
        )

    def halves(block, role):
        links.arrive(cot_all.at[block, pl.ds(0, ROWS // 2)], role, y_down)
        links.arrive(cot_all.at[block, pl.ds(ROWS // 2, ROWS // 2)], role + 1, y_up)

    project(part, first=True)
    forward(down, up, 13, 14, 15)
    project(down)
    project(up)
    links.arrive(cot_all.at[over], 12, far)
    links.send(cot_all.at[over], cot_all.at[over], 17, y_up)
    links.send(cot_all.at[over], cot_all.at[over], 18, y_down)
    project(over)
    relay(0)
    halves(across, 15)
    project(across)
    relay(1)
    down_over = down + 1 - 2 * high
    up_over = up + 1 - 2 * high
    across_over = across + 1 - 2 * high
    forward(down_over, up_over, 17, 18, 19)
    project(down_over)
    project(up_over)
    relay(2)
    halves(across_over, 19)
    project(across_over)
    dat_ref[...] = acc[...].astype(BF16)
    for n, (own, window) in enumerate(arrays):
        links.arrive(window.at[3 - 2 * core], 4 * n + 2, sibling)
        links.arrive(window.at[1 + 2 * core], 4 * n + 3, sibling)
    links.finish()


def gather(ids, keys, values, cotangent, weight):
    return pl.pallas_call(
        gather_kernel,
        out_shape=(
            jax.ShapeDtypeStruct((WINDOW, 2, CHUNK), jnp.int32),
            jax.ShapeDtypeStruct((WINDOW, ROWS, COLS), BF16),
            jax.ShapeDtypeStruct((WINDOW, ROWS, COLS), BF16),
            jax.ShapeDtypeStruct((TP, ROWS, COLS), BF16),
            jax.ShapeDtypeStruct((ROWS, COLS), BF16),
        ),
        in_specs=[VMEM] * 5,
        out_specs=(VMEM,) * 5,
        scratch_shapes=[
            pltpu.VMEM((ROWS, COLS), F32),
            pltpu.SemaphoreType.DMA((21,)),
            pltpu.SemaphoreType.DMA((21,)),
        ],
        compiler_params=pltpu.CompilerParams(
            collective_id=0, has_side_effects=True, vmem_limit_bytes=LIMIT
        ),
        name="gather",
    )(ids, keys, values, cotangent, weight)


def dot(a, b, contract):
    return lax.dot_general(a, b, ((contract[:1], contract[1:]), ((), ())), preferred_element_type=F32)


def local_kernel(
    ids_smem, ids_col, ids_row, q_ref, k_ref, v_ref, dat_ref, cot_ref, w_ref,
    mixed_ref, wpart_ref, dq_ref, dkv_ref, own_ref,
    kept, out_acc, dq_acc, dk_acc, dv_acc, att,
):
    dk_acc[...] = jnp.zeros_like(dk_acc)
    dv_acc[...] = jnp.zeros_like(dv_acc)
    for qc in range(ROWS // CHUNK):
        rows = pl.ds(qc * CHUNK, CHUNK)
        q_first, q_last = ids_smem[OWN, qc, 0], ids_smem[OWN, qc, CHUNK - 1]
        lo, hi = jnp.int32(KEY_CHUNKS), jnp.int32(0)
        for kc in range(KEY_CHUNKS):
            s, r = kc // 2, kc % 2
            meets = (ids_smem[s, r, CHUNK - 1] >= q_first) & (ids_smem[s, r, 0] <= q_last)
            lo = jnp.minimum(lo, jnp.where(meets, kc, KEY_CHUNKS))
            hi = jnp.maximum(hi, jnp.where(meets, kc + 1, 0))
        q_ids = jnp.concatenate([ids_col[rows, :]] * (CHUNK // 128), axis=1)
        for h in range(HEADS_DEV):
            cols = pl.ds(h * HEAD, HEAD)
            q = q_ref[rows, cols]
            g = dat_ref[rows, cols]

            def keys_at(kc):
                return pl.ds(pl.multiple_of(kc * CHUNK, CHUNK), CHUNK)

            def score(kc, top):
                s = dot(q, k_ref[keys_at(kc), cols], (1, 1))
                k_ids = ids_row[lax.div(kc, 2), pl.ds(lax.rem(kc, 2), 1), :]
                s = jnp.where(q_ids == k_ids, s, NEG)
                kept[kc] = s
                return jnp.maximum(top, jnp.maximum(s[:, :128], s[:, 128:]))

            top = lax.fori_loop(lo, hi, score, jnp.full((CHUNK, 128), NEG, F32))
            top = jnp.max(top, axis=1, keepdims=True) * EXP2_SCALE
            top = jnp.broadcast_to(top, (CHUNK, CHUNK))
            out_acc[...] = jnp.zeros_like(out_acc)

            def attend(kc, total):
                p = jnp.exp2(kept[kc] * EXP2_SCALE - top)
                kept[kc] = p
                out_acc[...] += dot(p.astype(BF16), v_ref[keys_at(kc), cols], (1, 0))
                return total + (p[:, :128] + p[:, 128:])

            total = lax.fori_loop(lo, hi, attend, jnp.zeros((CHUNK, 128), F32))
            inverse = 1.0 / jnp.sum(total, axis=1, keepdims=True)
            attended = (out_acc[...] * inverse).astype(BF16)
            att[rows, cols] = attended
            delta = jnp.sum(g.astype(F32) * attended.astype(F32), axis=1, keepdims=True)
            inverse = jnp.broadcast_to(inverse, (CHUNK, CHUNK))
            delta = jnp.broadcast_to(delta, (CHUNK, CHUNK))
            dq_acc[...] = jnp.zeros_like(dq_acc)

            def back(kc, carry):
                here = keys_at(kc)
                k = k_ref[here, cols]
                dots = dot(g, v_ref[here, cols], (1, 1))
                weight = kept[kc] * inverse
                dscores = (weight * (dots - delta)).astype(BF16)
                dv_acc[here, cols] += dot(weight.astype(BF16), g, (0, 0))
                dk_acc[here, cols] += dot(dscores, q, (0, 0))
                dq_acc[...] += dot(dscores, k, (1, 0))
                return carry

            lax.fori_loop(lo, hi, back, 0)
            dq_ref[rows, cols] = (dq_acc[...] * SCALE).astype(BF16)
    for block in range(TP):
        cols = pl.ds(block * COLS, COLS)
        mixed_ref[block] = dot(att[...], w_ref[:, cols], (1, 0)).astype(BF16)
        term = dot(att[...], cot_ref[block], (0, 0)).astype(BF16)
        half = pl.ds((block % 2) * COLS, COLS)
        for c in range(2):
            for z in range(4):
                first = c * 192 + z * PIECE_ROWS
                wpart_ref[c, block // 2, z, :, half] = term[first : first + PIECE_ROWS]
    for s in range(WINDOW):
        here = pl.ds(s * ROWS, ROWS)
        if s == OWN:
            own_ref[0] = dk_acc[here, :] * SCALE
            own_ref[1] = dv_acc[here, :]
        else:
            dkv_ref[s, 0] = (dk_acc[here, :] * SCALE).astype(BF16)
            dkv_ref[s, 1] = dv_acc[here, :].astype(BF16)


def local(ids_all, ids_col, query, k_all, v_all, d_att, cot_all, weight):
    flat = (WINDOW * ROWS, COLS)
    return pl.pallas_call(
        local_kernel,
        out_shape=(
            jax.ShapeDtypeStruct((TP, ROWS, COLS), BF16),
            jax.ShapeDtypeStruct((2, 4, 4, PIECE_ROWS, PIECE_COLS), BF16),
            jax.ShapeDtypeStruct((ROWS, COLS), BF16),
            jax.ShapeDtypeStruct((WINDOW, 2, ROWS, COLS), BF16),
            jax.ShapeDtypeStruct((2, ROWS, COLS), F32),
        ),
        in_specs=[SMEM] + [VMEM] * 8,
        out_specs=(VMEM,) * 5,
        scratch_shapes=[
            pltpu.VMEM((KEY_CHUNKS, CHUNK, CHUNK), F32),
            pltpu.VMEM((CHUNK, HEAD), F32),
            pltpu.VMEM((CHUNK, HEAD), F32),
            pltpu.VMEM(flat, F32),
            pltpu.VMEM(flat, F32),
            pltpu.VMEM((ROWS, COLS), BF16),
        ],
        compiler_params=pltpu.CompilerParams(vmem_limit_bytes=LIMIT),
        name="local",
    )(
        ids_all, ids_col, ids_all, query, k_all.reshape(flat), v_all.reshape(flat),
        d_att, cot_all, weight,
    )


def reduce_kernel(
    m_ref, w_ref, dkv_ref, own_ref,
    mixed_ref, gk_ref, gv_ref, gw_ref,
    dkv_in, dkv_out, m_hop, m_in, m_out, m_far,
    w_core, w_sum, w_hop, w_in, w_x, w_z, w_all,
    send_sem, recv_sem,
):
    place = lax.axis_index("ctx")
    part = lax.axis_index("tp")
    core = lax.rem(place, 2)
    z = lax.rem(lax.div(place, 2), 4)
    x = lax.div(place, 8)
    high = lax.rem(part, 2)
    after, before = ctx_ring(place, 2), ctx_ring(place, -2)
    sibling = {"ctx": place + 1 - 2 * core}
    x_up, x_down = ctx_ring(place, 8), ctx_ring(place, -8)
    z_to = [{"ctx": 8 * x + 2 * lax.rem(z + d, 4) + core} for d in (1, 2, 3)]
    z_from = [{"ctx": 8 * x + 2 * lax.rem(z + 4 - d, 4) + core} for d in (1, 2, 3)]
    up, down = lax.rem(part + 2, TP), lax.rem(part + 6, TP)
    over = part + 1 - 2 * high
    across = lax.rem(part + 4, TP)
    y_up, y_down, far = {"tp": up}, {"tp": down}, {"tp": over}
    greet([after, before, sibling, x_up, x_down, y_up, y_down, far] + z_to)
    links = Links(send_sem, recv_sem)
    low, top = pl.ds(0, ROWS // 2), pl.ds(ROWS // 2, ROWS // 2)
    z_low, z_top = pl.ds(0, 2), pl.ds(2, 2)
    flip = 1 - 2 * high

    links.send(dkv_ref.at[1 + 2 * core], dkv_in.at[1], 1, sibling)
    links.send(w_ref.at[1 - core], w_core, 4, sibling)
    links.send(dkv_ref.at[3 - 2 * core], dkv_in.at[0], 0, sibling)

    planes = ((1, flip), (0, 0))
    for n, add in planes:
        links.send(m_ref.at[across + add, low], m_hop.at[n, 0], 10 + 10 * n, y_up)
        links.send(m_ref.at[across + add, top], m_hop.at[n, 1], 11 + 10 * n, y_down)
    for n, add in planes:
        links.send(m_ref.at[up + add, top], m_in.at[n, 0, top], 12 + 10 * n, y_up)
        links.send(m_ref.at[down + add, low], m_in.at[n, 1, low], 13 + 10 * n, y_down)
    direct = 4 * core

    @pl.when(core == 0)
    def _():
        links._copy(dkv_ref.at[0], dkv_in.at[2], 2, before).start()

    @pl.when(core == 1)
    def _():
        links._copy(dkv_ref.at[4], dkv_in.at[3], 3, after).start()

    links.arrive(dkv_in.at[1], 1, sibling)
    summed = 4 - direct
    for n in range(2):
        dkv_out[n] = (dkv_ref[summed, n].astype(F32) + dkv_in[1, n].astype(F32)).astype(BF16)

    @pl.when(core == 0)
    def _():
        links._copy(dkv_out, dkv_in.at[3], 3, after).start()

    @pl.when(core == 1)
    def _():
        links._copy(dkv_out, dkv_in.at[2], 2, before).start()

    links.arrive(w_core, 4, sibling)

    def add_cores(i, carry):
        w_sum[i] = (w_ref[core, i].astype(F32) + w_core[i].astype(F32)).astype(BF16)
        return carry

    def quarter(step):
        return lax.rem(x + step, 4)

    lax.fori_loop(0, 4, add_cores, 0)
    links.send(w_sum.at[quarter(2), z_low], w_hop.at[0], 30, x_up)
    links.send(w_sum.at[quarter(2), z_top], w_hop.at[1], 31, x_down)
    links.send(w_sum.at[quarter(1), z_top], w_in.at[0, z_top], 32, x_up)
    links.send(w_sum.at[quarter(3), z_low], w_in.at[1, z_low], 33, x_down)

    for n, add in planes:
        links.arrive(m_hop.at[n, 0], 10 + 10 * n, y_down)
        m_out[n, 0] = (m_ref[up + add, low].astype(F32) + m_hop[n, 0].astype(F32)).astype(BF16)
        links.send(m_out.at[n, 0], m_in.at[n, 0, low], 14 + 10 * n, y_up)
        links.arrive(m_hop.at[n, 1], 11 + 10 * n, y_up)
        m_out[n, 1] = (m_ref[down + add, top].astype(F32) + m_hop[n, 1].astype(F32)).astype(BF16)
        links.send(m_out.at[n, 1], m_in.at[n, 1, top], 15 + 10 * n, y_down)

    links.arrive(w_hop.at[0], 30, x_down)
    w_hop[0] = (w_sum[quarter(1), z_low].astype(F32) + w_hop[0].astype(F32)).astype(BF16)
    links.send(w_hop.at[0], w_in.at[0, z_low], 34, x_up)
    links.arrive(w_hop.at[1], 31, x_up)
    w_hop[1] = (w_sum[quarter(3), z_top].astype(F32) + w_hop[1].astype(F32)).astype(BF16)
    links.send(w_hop.at[1], w_in.at[1, z_top], 35, x_down)
    links.arrive(w_in.at[0, z_top], 32, x_down)
    links.arrive(w_in.at[1, z_low], 33, x_up)
    links.arrive(w_in.at[0, z_low], 34, x_down)
    links.arrive(w_in.at[1, z_top], 35, x_up)

    def add_x(i, carry):
        w_x[i] = (
            w_sum[x, i].astype(F32) + w_in[0, i].astype(F32) + w_in[1, i].astype(F32)
        ).astype(BF16)
        return carry

    lax.fori_loop(0, 4, add_x, 0)
    for d in range(3):
        links.send(w_x.at[lax.rem(z + d + 1, 4)], w_z.at[d], 36 + d, z_to[d])

    def along_y(n, add):
        links.arrive(m_in.at[n, 0, top], 12 + 10 * n, y_down)
        links.arrive(m_in.at[n, 1, low], 13 + 10 * n, y_up)
        links.arrive(m_in.at[n, 0, low], 14 + 10 * n, y_down)
        links.arrive(m_in.at[n, 1, top], 15 + 10 * n, y_up)
        return m_ref[part + add].astype(F32) + m_in[n, 0].astype(F32) + m_in[n, 1].astype(F32)

    def total_z():
        for d in range(3):
            links.arrive(w_z.at[d], 36 + d, z_from[d])
        w_all[core, x, z] = (
            w_x[z].astype(F32)
            + w_z[0].astype(F32)
            + w_z[1].astype(F32)
            + w_z[2].astype(F32)
        ).astype(BF16)
        for d in range(3):
            links.send(w_all.at[core, x, z], w_all.at[core, x, z], 39 + d, z_to[d])

    total_z()
    m_far[0] = along_y(1, flip).astype(BF16)
    links.send(m_far.at[0], m_far.at[1], 16, far)

    for d in range(3):
        links.arrive(w_all.at[core, x, lax.rem(z + 3 - d, 4)], 39 + d, z_from[d])
    links.send(w_all.at[core, x], w_all.at[core, x], 42, x_up)
    links.send(w_all.at[core, x], w_all.at[core, x], 43, x_down)
    links.send(w_all.at[core, x], w_all.at[core, x], 46, sibling)
    below, above, opposite = quarter(3), quarter(1), quarter(2)
    links.arrive(w_all.at[core, below], 42, x_down)
    links.send(w_all.at[core, below, z_low], w_all.at[core, below, z_low], 44, x_up)
    links.arrive(w_all.at[core, above], 43, x_up)
    links.send(w_all.at[core, above, z_top], w_all.at[core, above, z_top], 45, x_down)
    links.send(w_all.at[core, below], w_all.at[core, below], 47, sibling)
    links.send(w_all.at[core, above], w_all.at[core, above], 48, sibling)

    m_in[0, 0] = along_y(0, 0).astype(BF16)
    links.arrive(dkv_in.at[0], 0, sibling)
    links.arrive(dkv_in.at[2], 2, after)
    links.arrive(dkv_in.at[3], 3, before)
    for n, out in enumerate((gk_ref, gv_ref)):
        out[...] = (
            own_ref[n]
            + dkv_in[0, n].astype(F32)
            + dkv_in[2, n].astype(F32)
            + dkv_in[3, n].astype(F32)
        ).astype(BF16)

    links.arrive(w_all.at[core, opposite, z_low], 44, x_down)
    links.arrive(w_all.at[core, opposite, z_top], 45, x_up)
    links.send(w_all.at[core, opposite], w_all.at[core, opposite], 49, sibling)
    links.arrive(m_far.at[1], 16, far)
    mixed_ref[...] = (m_in[0, 0].astype(F32) + m_far[1].astype(F32)).astype(BF16)
    other = 1 - core
    for role, block in ((46, x), (47, below), (48, above), (49, opposite)):
        links.arrive(w_all.at[other, block], role, sibling)
    for c in range(2):
        for i in range(4):
            for j in range(4):
                gw_ref[
                    pl.ds(c * 192 + j * PIECE_ROWS, PIECE_ROWS), pl.ds(i * PIECE_COLS, PIECE_COLS)
                ] = w_all[c, i, j]
    links._copy(dkv_out, dkv_in.at[2], 2, before).wait_send()
    links._copy(dkv_out, dkv_in.at[3], 3, after).wait_send()
    links.finish()


def reduce(m_part, w_part, dkv, own):
    block = (ROWS, COLS)
    return pl.pallas_call(
        reduce_kernel,
        out_shape=(
            jax.ShapeDtypeStruct(block, BF16),
            jax.ShapeDtypeStruct(block, BF16),
            jax.ShapeDtypeStruct(block, BF16),
            jax.ShapeDtypeStruct((COLS, FEATURES), BF16),
        ),
        in_specs=[VMEM] * 4,
        out_specs=(VMEM,) * 4,
        scratch_shapes=[
            pltpu.VMEM((4, 2, ROWS, COLS), BF16),
            pltpu.VMEM((2, ROWS, COLS), BF16),
            pltpu.VMEM((2, 2, ROWS // 2, COLS), BF16),
            pltpu.VMEM((2, 2, ROWS, COLS), BF16),
            pltpu.VMEM((2, 2, ROWS // 2, COLS), BF16),
            pltpu.VMEM((2, ROWS, COLS), BF16),
            pltpu.VMEM((4, 4, PIECE_ROWS, PIECE_COLS), BF16),
            pltpu.VMEM((4, 4, PIECE_ROWS, PIECE_COLS), BF16),
            pltpu.VMEM((2, 2, PIECE_ROWS, PIECE_COLS), BF16),
            pltpu.VMEM((2, 4, PIECE_ROWS, PIECE_COLS), BF16),
            pltpu.VMEM((4, PIECE_ROWS, PIECE_COLS), BF16),
            pltpu.VMEM((3, PIECE_ROWS, PIECE_COLS), BF16),
            pltpu.VMEM((2, 4, 4, PIECE_ROWS, PIECE_COLS), BF16),
            pltpu.SemaphoreType.DMA((50,)),
            pltpu.SemaphoreType.DMA((50,)),
        ],
        compiler_params=pltpu.CompilerParams(
            collective_id=1, has_side_effects=True, vmem_limit_bytes=LIMIT
        ),
        name="reduce",
    )(m_part, w_part, dkv, own)


def on_device(query, keys, values, image_ids, out_weight, cotangent):
    ids_col = jnp.broadcast_to(image_ids[:, None], (ROWS, 128))
    ids_all, k_all, v_all, cot_all, d_att = gather(
        image_ids.reshape(2, CHUNK), keys, values, cotangent, out_weight
    )
    m_part, w_part, grad_query, dkv, own = local(
        ids_all, ids_col, query, k_all, v_all, d_att, cot_all, out_weight
    )
    mixed, grad_keys, grad_values, grad_weight = reduce(m_part, w_part, dkv, own)
    return (mixed, grad_query, grad_keys, grad_values, grad_weight)


def solution(mesh):
    placed = (
        P("ctx", "tp"),
        P("ctx", "tp"),
        P("ctx", "tp"),
        P("ctx"),
        P("tp", None),
        P("ctx", "tp"),
    )
    return jax.shard_map(
        on_device,
        mesh=mesh,
        in_specs=placed,
        out_specs=(P("ctx", "tp"), P("ctx", "tp"), P("ctx", "tp"), P("ctx", "tp"), P("tp", None)),
        check_vma=False,
    )
```

time: 513 us -> 216 us (0.42)
  the two profiles are of different devices: /device:TPU:199 before, /device:TPU:41 now
where the time goes in v1:
time: 216 us; the launch traced here: 215 us
  Pallas kernels  205 us (95%)
  local copies, waits for them, and re-layouts  9.69 us (4%)
    pallas_call x1, Pallas kernels, reduce(): pl.pallas_call(reduce_kernel, out_shape=(jax.ShapeDtypeStruct(block, BF16...  98.5 us
    pallas_call x1, Pallas kernels, gather(): pl.pallas_call(gather_kernel, out_shape=(jax.ShapeDtypeStruct((WINDOW, 2,...  65.7 us
    pallas_call x1, Pallas kernels, local(): pl.pallas_call(local_kernel, out_shape=(jax.ShapeDtypeStruct((TP, ROWS, C...  40.8 us
    unnamed x6, local copies, waits for them, and re-layouts  6.9 us

profile of v1, /device:TPU:41, one launch (start us, length us, event | category | flops | bytes accessed | tf_op | source)
XLA Modules:
  0.0 215.4 jit_solution(2835614605614417298)
XLA Ops:
  0.6 1.3 reshape.20.ids_ref
  1.9 1.5 broadcast_in_dim.2.ids_col
  3.4 65.7 %gather.1 = (s32[5,2,256]{2,1,0:T(2,128)}, bf16[5,512,384]{2,1,0:T(8,128)(2,1)}, bf16[5,512,384]{2,1,0:T(8,128)(2,1)}, bf16[8,512,384]{2,1,0:T(8,128)(2,1)}, bf16[512,384]{1,0:T(8,128)(2,1)}) custom-call(s32[2,256]{1,0:T(2,128)} %reshape.20.ids_ref, bf16[512,384]{1,0:T(8,128)(2,1)} %k_ref.1, bf16[512,384]{1,0:T(8,128)(2,1)} %v_ref.1, ...), custom_call_target="tpu_custom_call" | custom-call | tf_op jit(solution)/shard_map/gather/pallas_call | solution.py:175
  69.1 40.8 %local.1 = (bf16[8,512,384]{2,1,0:T(8,128)(2,1)}, bf16[2,4,4,48,768]{4,3,2,1,0:T(8,128)(2,1)}, bf16[512,384]{1,0:T(8,128)(2,1)}, bf16[5,2,512,384]{3,2,1,0:T(8,128)(2,1)}, f32[2,512,384]{2,1,0:T(8,128)}) custom-call(s32[5,2,256]{2,1,0:T(2,128)} %get-tuple-element.19.ids_smem.ids_row, s32[512,128]{1,0:T(8,128)} %broadcast_in_dim.2.ids_col, ...), custom_call_target="tpu_custom_call" | custom-call | tf_op jit(solution)/shard_map/local/pallas_call | solution.py:288
  109.9 98.5 %reduce.1 = (bf16[512,384]{1,0:T(8,128)(2,1)}, bf16[512,384]{1,0:T(8,128)(2,1)}, bf16[512,384]{1,0:T(8,128)(2,1)}, bf16[384,3072]{1,0:T(8,128)(2,1)}) custom-call(bf16[8,512,384]{2,1,0:T(8,128)(2,1)} %get-tuple-element.24.m_ref, bf16[2,4,4,48,768]{4,3,2,1,0:T(8,128)(2,1)} %get-tuple-element.25.w_ref, bf16[5,2,512,384]{3,2,1,0:T(8,128)(2,1)} %get-tuple-element.26.dkv_ref, ...), custom_call_target="tpu_custom_call" | custom-call | tf_op jit(solution)/shard_map/reduce/pallas_call | solution.py:490
  208.4 0.0 copy-start
  208.5 1.9 copy.15
  210.4 1.8 copy.16
  212.2 1.8 copy.17
  214.0 0.0 copy-done
  214.0 1.4 copy.18
Async XLA Ops:
  208.4 5.5 %copy-start = (bf16[384,3072]{1,0:T(8,128)(2,1)S(1)}, bf16[384,3072]{1,0:T(8,128)(2,1)}, u32[]{:S(2)}) copy-start(bf16[384,3072]{1,0:T(8,128)(2,1)} %get-tuple-element.42) | copy-start | bytes 7077892

commit v2 on v0

v2 whole, which is shorter than its diff:
```python
import functools

import jax
import jax.numpy as jnp
from jax import lax
from jax.experimental import pallas as pl
from jax.experimental.pallas import tpu as pltpu
from jax.sharding import PartitionSpec as P

HEAD = 128
ROWS = 512
COLS = 384
HEADS_DEV = COLS // HEAD
TP = 8
FEATURES = TP * COLS
WINDOW = 5
OWN = 2
CHUNK = 256
HALF = ROWS // 2
PIECE_ROWS = 48
PIECE_COLS = 768
NEG = -1e30
SCALE = HEAD ** -0.5
EXP2_SCALE = SCALE * 1.4426950408889634
F32 = jnp.float32
BF16 = jnp.bfloat16
MESH = pl.DeviceIdType.MESH
VMEM = pl.BlockSpec(memory_space=pltpu.VMEM)
ANY = pl.BlockSpec(memory_space=pl.ANY)
LIMIT = 60 * 1024 * 1024


class Links:
    def __init__(self, send_sem, recv_sem):
        self.send_sem, self.recv_sem = send_sem, recv_sem
        self.sent = []

    def _copy(self, src, dst, role, where):
        return pltpu.make_async_remote_copy(
            src_ref=src,
            dst_ref=dst,
            send_sem=self.send_sem.at[role],
            recv_sem=self.recv_sem.at[role],
            device_id=where,
            device_id_type=MESH,
        )

    def send(self, src, dst, role, where, keep=True):
        copy = self._copy(src, dst, role, where)
        copy.start()
        if keep:
            self.sent.append(copy)

    def arrive(self, dst, role, where):
        self._copy(dst, dst, role, where).wait_recv()

    def left(self, src, role, where):
        self._copy(src, src, role, where).wait_send()

    def finish(self):
        for copy in self.sent:
            copy.wait_send()


def greet(peers):
    barrier = pltpu.get_barrier_semaphore()
    for where in peers:
        pl.semaphore_signal(barrier, inc=1, device_id=where, device_id_type=MESH)
    pl.semaphore_wait(barrier, len(peers))


def ctx_ring(place, step):
    return {"ctx": lax.rem(place + step + 32, 32)}


def columns(index):
    return pl.ds(pl.multiple_of(index * COLS, COLS), COLS)


IDS, KV, COT, DKV, MIX, FAR, CORE, XR, ZR, ZG, XG, CG, ROLES = (
    0, 4, 16, 25, 37, 49, 50, 54, 60, 63, 66, 70, 74,
)


def dot(a, b, contract):
    return lax.dot_general(
        a, b, ((contract[:1], contract[1:]), ((), ())), preferred_element_type=F32
    )


def wide(x, times):
    return jnp.concatenate([x] * times, axis=1)


def head_columns(h):
    return pl.ds(pl.multiple_of(h * HEAD, HEAD), HEAD)


def sublayer_kernel(
    ids_ref, ids_col, q_ref, k_ref, v_ref, cot_ref, w_ref,
    mixed_ref, gq_ref, gk_ref, gv_ref, gw_ref,
    ids_all, kv_all, cot_all, d_att, d_acc,
    top_ref, total_ref, out_acc, lse_ref, delta_ref, dq_acc, att, att_t,
    dkv, own, dkv_in,
    m_ref, m_hop, m_in, m_out, m_far,
    w_part, w_core, w_sum, w_hop, w_in, w_x, w_z, w_all,
    send_sem, recv_sem,
):
    place = lax.axis_index("ctx")
    part = lax.axis_index("tp")
    core = lax.rem(place, 2)
    z = lax.rem(lax.div(place, 2), 4)
    x = lax.div(place, 8)
    high = lax.rem(part, 2)
    flip = 1 - 2 * high
    after, before = ctx_ring(place, 2), ctx_ring(place, -2)
    sibling = {"ctx": place + 1 - 2 * core}
    x_up, x_down = ctx_ring(place, 8), ctx_ring(place, -8)
    z_to = [{"ctx": 8 * x + 2 * lax.rem(z + d, 4) + core} for d in (1, 2, 3)]
    z_from = [{"ctx": 8 * x + 2 * lax.rem(z + 4 - d, 4) + core} for d in (1, 2, 3)]
    up, down = lax.rem(part + 2, TP), lax.rem(part + 6, TP)
    across = lax.rem(part + 4, TP)
    over = part + flip
    y_up, y_down, far = {"tp": up}, {"tp": down}, {"tp": over}
    low, top = pl.ds(0, HALF), pl.ds(HALF, HALF)
    z_low, z_top = pl.ds(0, 2), pl.ds(2, 2)
    sib_slot, relay_slot = 3 - 2 * core, 1 + 2 * core
    direct_slot, sum_slot = 4 * core, 4 - 4 * core
    direct_to = {"ctx": lax.rem(place + 30 + 4 * core, 32)}
    sum_to = {"ctx": lax.rem(place + 34 - 4 * core, 32)}

    kv_all[OWN, 0] = k_ref[...]
    kv_all[OWN, 1] = v_ref[...]
    greet([after, before, sibling, x_up, x_down, y_up, y_down, far] + z_to)
    links = Links(send_sem, recv_sem)

    links.send(cot_ref, cot_all.at[part], COT, far)
    links.send(cot_ref, cot_all.at[part], COT + 1, y_up)
    links.send(cot_ref, cot_all.at[part], COT + 2, y_down)
    links.send(ids_ref, ids_all.at[0], IDS, after)
    links.send(ids_ref, ids_all.at[4], IDS + 1, before)
    links.send(ids_ref, ids_all.at[relay_slot], IDS + 2, sibling)

    def send_heads(h, carry):
        mine = kv_all.at[OWN, :, :, head_columns(h)]
        role = KV + 4 * h
        links.send(mine, kv_all.at[0, :, :, head_columns(h)], role, after, False)
        links.send(mine, kv_all.at[4, :, :, head_columns(h)], role + 1, before, False)
        links.send(mine, kv_all.at[relay_slot, :, :, head_columns(h)], role + 2, sibling, False)
        return carry

    lax.fori_loop(0, HEADS_DEV, send_heads, 0)
    ids_all[OWN] = ids_ref[...]
    cot_all[part] = cot_ref[...]

    def project(block, first=False):
        term = dot(cot_all[block], w_ref[:, columns(block)], (1, 1))
        if first:
            d_acc[...] = term
        else:
            d_acc[...] += term

    def key_ids(slot):
        return jnp.concatenate([ids_all[slot, 0:1, :], ids_all[slot, 1:2, :]], axis=1)

    def scores(h, slot):
        cols = head_columns(h)
        s = dot(q_ref[:, cols], kv_all[slot, 0, :, cols], (1, 1)) * EXP2_SCALE
        return jnp.where(wide(ids_col[...], ROWS // 128) == key_ids(slot), s, NEG)

    def lanes(op, s):
        return functools.reduce(op, [s[:, n : n + 128] for n in range(0, ROWS, 128)])

    def attend(h, slot, first=False):
        s = scores(h, slot)
        peak = jnp.max(lanes(jnp.maximum, s), axis=1, keepdims=True)
        peak = jnp.broadcast_to(peak, (ROWS, 128))
        if not first:
            old = top_ref[h]
            peak = jnp.maximum(old, peak)
            fade = jnp.exp2(old - peak)
        p = jnp.exp2(s - wide(peak, ROWS // 128))
        part_total = lanes(jnp.add, p)
        term = dot(p.astype(BF16), kv_all[slot, 1, :, head_columns(h)], (1, 0))
        if not first:
            part_total += total_ref[h] * fade
            term += out_acc[h] * fade
        total_ref[h] = part_total
        out_acc[h] = term
        top_ref[h] = peak

    def settle(h):
        cols = head_columns(h)
        total = jnp.sum(total_ref[h], axis=1, keepdims=True)
        attended = out_acc[h] * (1.0 / total)
        att_t[cols, :] = jnp.transpose(attended).astype(BF16)
        attended = attended.astype(BF16)
        att[:, cols] = attended
        lse_ref[...] = top_ref[h] + jnp.broadcast_to(jnp.log2(total), (ROWS, 128))
        delta = jnp.sum(
            attended.astype(F32) * d_att[:, cols].astype(F32), axis=1, keepdims=True
        )
        delta_ref[...] = jnp.broadcast_to(delta, (ROWS, 128))

    def back(h, slot, first=False, last=False):
        cols = head_columns(h)
        q, g = q_ref[:, cols], d_att[:, cols]
        k, v = kv_all[slot, 0, :, cols], kv_all[slot, 1, :, cols]
        weight = jnp.exp2(scores(h, slot) - wide(lse_ref[...], ROWS // 128))
        dots = dot(g, v, (1, 1))
        dscores = (weight * (dots - wide(delta_ref[...], ROWS // 128))).astype(BF16)
        dk = dot(dscores, q, (0, 0)) * SCALE
        dv = dot(weight.astype(BF16), g, (0, 0))
        dq = dot(dscores, k, (1, 0))
        if not first:
            dq += dq_acc[...]
        if last:
            own[0, :, cols] = dk
            own[1, :, cols] = dv
            gq_ref[:, cols] = (dq * SCALE).astype(BF16)
        else:
            dkv[slot, 0, :, cols] = dk.astype(BF16)
            dkv[slot, 1, :, cols] = dv.astype(BF16)
            dq_acc[...] = dq

    def each_head(work):
        def step(h, carry):
            work(h)
            return carry

        lax.fori_loop(0, HEADS_DEV, step, 0)

    def pass_on(low_block, high_block, low_role, high_role, role):
        links.arrive(cot_all.at[low_block], low_role, y_down)
        links.send(cot_all.at[low_block, low], cot_all.at[low_block, low], role, y_up, False)
        links.arrive(cot_all.at[high_block], high_role, y_up)
        links.send(
            cot_all.at[high_block, top], cot_all.at[high_block, top], role + 1, y_down, False
        )

    def halves(block, role):
        links.arrive(cot_all.at[block, low], role, y_down)
        links.arrive(cot_all.at[block, top], role + 1, y_up)

    project(part, first=True)
    each_head(lambda h: attend(h, OWN, first=True))
    pass_on(down, up, COT + 1, COT + 2, COT + 3)
    project(down)
    project(up)
    links.arrive(ids_all.at[0], IDS, before)
    links.arrive(ids_all.at[4], IDS + 1, after)
    links.send(ids_all.at[sum_slot], ids_all.at[sib_slot], IDS + 3, sibling)
    links.arrive(cot_all.at[over], COT, far)
    links.send(cot_all.at[over], cot_all.at[over], COT + 5, y_up)
    links.send(cot_all.at[over], cot_all.at[over], COT + 6, y_down)
    project(over)
    links.arrive(ids_all.at[sib_slot], IDS + 2, sibling)

    def attend_sibling(h):
        links.arrive(kv_all.at[sib_slot, :, :, head_columns(h)], KV + 4 * h + 2, sibling)
        attend(h, sib_slot)

    each_head(attend_sibling)
    halves(across, COT + 3)
    project(across)
    links.arrive(ids_all.at[relay_slot], IDS + 3, sibling)

    def rest_of_cotangent():
        down_over, up_over, across_over = down + flip, up + flip, across + flip
        pass_on(down_over, up_over, COT + 5, COT + 6, COT + 7)
        project(down_over)
        project(up_over)
        halves(across_over, COT + 7)
        project(across_over)
        d_att[...] = d_acc[...].astype(BF16)

    planes = ((1, flip), (0, 0))

    def share_heads():
        def mix(block):
            m_ref[block] = dot(att[...], w_ref[:, columns(block)], (1, 0)).astype(BF16)

        for n, add in planes:
            mix(across + add)
            role = MIX + 6 * n
            links.send(m_ref.at[across + add, low], m_hop.at[n, 0], role, y_up, False)
            links.send(m_ref.at[across + add, top], m_hop.at[n, 1], role + 1, y_down, False)

        def quarter_weight(n, carry):
            for side in range(2):
                term = dot(att_t[...], cot_all[2 * n + side], (1, 0)).astype(BF16)
                side_cols = pl.ds(side * COLS, COLS)
                for c in range(2):
                    for j in range(4):
                        first = c * 192 + j * PIECE_ROWS
                        w_part[c, n, j, :, side_cols] = term[first : first + PIECE_ROWS]
            links.send(w_part.at[1 - core, n], w_core.at[n], CORE + n, sibling, False)
            return carry

        lax.fori_loop(0, 4, quarter_weight, 0)
        for n, add in planes:
            mix(up + add)
            mix(down + add)
            role = MIX + 6 * n
            links.send(m_ref.at[up + add, top], m_in.at[n, 0, top], role + 2, y_up, False)
            links.send(m_ref.at[down + add, low], m_in.at[n, 1, low], role + 3, y_down, False)
        for n, add in planes:
            mix(part + add)

    def per_head(h):
        cols = head_columns(h)
        role = KV + 4 * h
        links.arrive(kv_all.at[0, :, :, cols], role, before)
        links.arrive(kv_all.at[4, :, :, cols], role + 1, after)
        links.send(
            kv_all.at[sum_slot, :, :, cols], kv_all.at[sib_slot, :, :, cols], role + 3, sibling,
            False,
        )
        attend(h, 0)
        attend(h, 4)
        pl.when(h == 0)(rest_of_cotangent)
        links.arrive(kv_all.at[relay_slot, :, :, cols], role + 3, sibling)
        attend(h, relay_slot)
        settle(h)
        pl.when(h == HEADS_DEV - 1)(share_heads)
        role = DKV + 4 * h
        back(h, relay_slot, first=True)
        links.send(
            dkv.at[relay_slot, :, :, cols], dkv_in.at[1, :, :, cols], role + 1, sibling, False
        )
        back(h, direct_slot)
        links.send(
            dkv.at[direct_slot, :, :, cols], dkv_in.at[2 + core, :, :, cols], role + 2 + core,
            direct_to, False,
        )
        back(h, sum_slot)
        links.arrive(dkv_in.at[1, :, :, cols], role + 1, sibling)
        for n in range(2):
            dkv[sum_slot, n, :, cols] = (
                dkv[sum_slot, n, :, cols].astype(F32) + dkv_in[1, n, :, cols].astype(F32)
            ).astype(BF16)
        links.send(
            dkv.at[sum_slot, :, :, cols], dkv_in.at[3 - core, :, :, cols], role + 3 - core,
            sum_to, False,
        )
        back(h, sib_slot)
        links.send(dkv.at[sib_slot, :, :, cols], dkv_in.at[0, :, :, cols], role, sibling, False)
        back(h, OWN, last=True)

    each_head(per_head)

    def quarter(step):
        return lax.rem(x + step, 4)

    def add_cores(i, carry):
        links.arrive(w_core.at[i], CORE + i, sibling)
        w_sum[i] = (w_part[core, i].astype(F32) + w_core[i].astype(F32)).astype(BF16)
        return carry

    lax.fori_loop(0, 4, add_cores, 0)
    links.send(w_sum.at[quarter(2), z_low], w_hop.at[0], XR, x_up)
    links.send(w_sum.at[quarter(2), z_top], w_hop.at[1], XR + 1, x_down)
    links.send(w_sum.at[quarter(1), z_top], w_in.at[0, z_top], XR + 2, x_up)
    links.send(w_sum.at[quarter(3), z_low], w_in.at[1, z_low], XR + 3, x_down)

    for n, add in planes:
        role = MIX + 6 * n
        links.arrive(m_hop.at[n, 0], role, y_down)
        m_out[n, 0] = (m_ref[up + add, low].astype(F32) + m_hop[n, 0].astype(F32)).astype(BF16)
        links.send(m_out.at[n, 0], m_in.at[n, 0, low], role + 4, y_up)
        links.arrive(m_hop.at[n, 1], role + 1, y_up)
        m_out[n, 1] = (m_ref[down + add, top].astype(F32) + m_hop[n, 1].astype(F32)).astype(BF16)
        links.send(m_out.at[n, 1], m_in.at[n, 1, top], role + 5, y_down)

    links.arrive(w_hop.at[0], XR, x_down)
    w_hop[0] = (w_sum[quarter(1), z_low].astype(F32) + w_hop[0].astype(F32)).astype(BF16)
    links.send(w_hop.at[0], w_in.at[0, z_low], XR + 4, x_up)
    links.arrive(w_hop.at[1], XR + 1, x_up)
    w_hop[1] = (w_sum[quarter(3), z_top].astype(F32) + w_hop[1].astype(F32)).astype(BF16)
    links.send(w_hop.at[1], w_in.at[1, z_top], XR + 5, x_down)
    links.arrive(w_in.at[0, z_top], XR + 2, x_down)
    links.arrive(w_in.at[1, z_low], XR + 3, x_up)
    links.arrive(w_in.at[0, z_low], XR + 4, x_down)
    links.arrive(w_in.at[1, z_top], XR + 5, x_up)

    def add_x(i, carry):
        w_x[i] = (
            w_sum[x, i].astype(F32) + w_in[0, i].astype(F32) + w_in[1, i].astype(F32)
        ).astype(BF16)
        return carry

    lax.fori_loop(0, 4, add_x, 0)
    for d in range(3):
        links.send(w_x.at[lax.rem(z + d + 1, 4)], w_z.at[d], ZR + d, z_to[d])

    def along_y(n, add):
        role = MIX + 6 * n
        links.arrive(m_in.at[n, 0, top], role + 2, y_down)
        links.arrive(m_in.at[n, 1, low], role + 3, y_up)
        links.arrive(m_in.at[n, 0, low], role + 4, y_down)
        links.arrive(m_in.at[n, 1, top], role + 5, y_up)
        return m_ref[part + add].astype(F32) + m_in[n, 0].astype(F32) + m_in[n, 1].astype(F32)

    for d in range(3):
        links.arrive(w_z.at[d], ZR + d, z_from[d])
    w_all[core, x, z] = (
        w_x[z].astype(F32) + w_z[0].astype(F32) + w_z[1].astype(F32) + w_z[2].astype(F32)
    ).astype(BF16)
    for d in range(3):
        links.send(w_all.at[core, x, z], w_all.at[core, x, z], ZG + d, z_to[d])

    m_far[0] = along_y(1, flip).astype(BF16)
    links.send(m_far.at[0], m_far.at[1], FAR, far)

    for d in range(3):
        links.arrive(w_all.at[core, x, lax.rem(z + 3 - d, 4)], ZG + d, z_from[d])
    links.send(w_all.at[core, x], w_all.at[core, x], XG, x_up)
    links.send(w_all.at[core, x], w_all.at[core, x], XG + 1, x_down)
    links.send(w_all.at[core, x], w_all.at[core, x], CG, sibling)
    below, above, opposite = quarter(3), quarter(1), quarter(2)
    links.arrive(w_all.at[core, below], XG, x_down)
    links.send(w_all.at[core, below, z_low], w_all.at[core, below, z_low], XG + 2, x_up)
    links.arrive(w_all.at[core, above], XG + 1, x_up)
    links.send(w_all.at[core, above, z_top], w_all.at[core, above, z_top], XG + 3, x_down)
    links.send(w_all.at[core, below], w_all.at[core, below], CG + 1, sibling)
    links.send(w_all.at[core, above], w_all.at[core, above], CG + 2, sibling)

    m_in[0, 0] = along_y(0, 0).astype(BF16)

    def add_keys(h):
        cols = head_columns(h)
        role = DKV + 4 * h
        links.arrive(dkv_in.at[0, :, :, cols], role, sibling)
        links.arrive(dkv_in.at[2, :, :, cols], role + 2, after)
        links.arrive(dkv_in.at[3, :, :, cols], role + 3, before)
        for n, out in enumerate((gk_ref, gv_ref)):
            out[:, cols] = (
                own[n, :, cols]
                + dkv_in[0, n, :, cols].astype(F32)
                + dkv_in[2, n, :, cols].astype(F32)
                + dkv_in[3, n, :, cols].astype(F32)
            ).astype(BF16)

    each_head(add_keys)
    links.arrive(w_all.at[core, opposite, z_low], XG + 2, x_down)
    links.arrive(w_all.at[core, opposite, z_top], XG + 3, x_up)
    links.send(w_all.at[core, opposite], w_all.at[core, opposite], CG + 3, sibling)
    links.arrive(m_far.at[1], FAR, far)
    mixed_ref[...] = (m_in[0, 0].astype(F32) + m_far[1].astype(F32)).astype(BF16)
    other = 1 - core
    for role, block in ((CG, x), (CG + 1, below), (CG + 2, above), (CG + 3, opposite)):
        links.arrive(w_all.at[other, block], role, sibling)
    for c in range(2):
        for i in range(4):
            for j in range(4):
                gw_ref[
                    pl.ds(c * 192 + j * PIECE_ROWS, PIECE_ROWS), pl.ds(i * PIECE_COLS, PIECE_COLS)
                ] = w_all[c, i, j]

    def heads_left(h):
        cols = head_columns(h)
        for n in range(4):
            links.left(kv_all.at[OWN, :, :, cols], KV + 4 * h + n, sibling)
            links.left(dkv.at[OWN, :, :, cols], DKV + 4 * h + n, sibling)

    each_head(heads_left)
    for n in range(2):
        for k in (0, 1, 2, 3):
            links.left(m_hop.at[n, 0], MIX + 6 * n + k, y_up)
    for n in range(4):
        links.left(w_core.at[n], CORE + n, sibling)
    for role in (3, 4, 7, 8):
        links.left(cot_all.at[0, low], COT + role, y_up)
    links.finish()


def sublayer(ids, ids_col, query, keys, values, cotangent, weight):
    block = (ROWS, COLS)
    bf16 = lambda *shape: pltpu.VMEM(shape, BF16)
    f32 = lambda *shape: pltpu.VMEM(shape, F32)
    heads = (HEADS_DEV, ROWS, HEAD)
    piece = (PIECE_ROWS, PIECE_COLS)
    return pl.pallas_call(
        sublayer_kernel,
        out_shape=tuple([jax.ShapeDtypeStruct(block, BF16)] * 4)
        + (jax.ShapeDtypeStruct((COLS, FEATURES), BF16),),
        in_specs=[VMEM] * 7,
        out_specs=(VMEM,) * 5,
        scratch_shapes=[
            pltpu.VMEM((WINDOW, 2, CHUNK), jnp.int32),
            bf16(WINDOW, 2, *block),
            bf16(TP, *block),
            bf16(*block),
            f32(*block),
            f32(*heads),
            f32(*heads),
            f32(*heads),
            f32(ROWS, HEAD),
            f32(ROWS, HEAD),
            f32(ROWS, HEAD),
            bf16(*block),
            bf16(COLS, ROWS),
            bf16(WINDOW, 2, *block),
            f32(2, *block),
            bf16(4, 2, *block),
            bf16(TP, *block),
            bf16(2, 2, HALF, COLS),
            bf16(2, 2, *block),
            bf16(2, 2, HALF, COLS),
            bf16(2, *block),
            bf16(2, 4, 4, *piece),
            bf16(4, 4, *piece),
            bf16(4, 4, *piece),
            bf16(2, 2, *piece),
            bf16(2, 4, *piece),
            bf16(4, *piece),
            bf16(3, *piece),
            bf16(2, 4, 4, *piece),
            pltpu.SemaphoreType.DMA((ROLES,)),
            pltpu.SemaphoreType.DMA((ROLES,)),
        ],
        compiler_params=pltpu.CompilerParams(
            collective_id=0, has_side_effects=True, vmem_limit_bytes=LIMIT
        ),
        name="sublayer",
    )(ids, ids_col, query, keys, values, cotangent, weight)


def hand_over_kernel(*refs):
    count = len(refs) // 2
    for n in range(count):
        refs[count + n][...] = refs[n][...]


def hand_over(arrays):
    return pl.pallas_call(
        hand_over_kernel,
        out_shape=tuple(jax.ShapeDtypeStruct(a.shape, a.dtype) for a in arrays),
        in_specs=[VMEM] * len(arrays),
        out_specs=(VMEM,) * len(arrays),
        name="hand_over",
    )(*arrays)


def on_device(query, keys, values, image_ids, out_weight, cotangent):
    ids_col = jnp.broadcast_to(image_ids[:, None], (ROWS, 128))
    return hand_over(
        sublayer(
            image_ids.reshape(2, CHUNK), ids_col, query, keys, values, cotangent, out_weight
        )
    )


def solution(mesh):
    placed = (
        P("ctx", "tp"),
        P("ctx", "tp"),
        P("ctx", "tp"),
        P("ctx"),
        P("tp", None),
        P("ctx", "tp"),
    )
    return jax.shard_map(
        on_device,
        mesh=mesh,
        in_specs=placed,
        out_specs=(P("ctx", "tp"), P("ctx", "tp"), P("ctx", "tp"), P("ctx", "tp"), P("tp", None)),
        check_vma=False,
    )
```

time: 513 us -> 154 us (0.30)
  the two profiles are of different devices: /device:TPU:199 before, /device:TPU:41 now
where the time goes in v2:
time: 154 us; the launch traced here: 153 us
  Pallas kernels  150 us (97%)
  local copies, waits for them, and re-layouts  2.79 us (2%)
    pallas_call x1, Pallas kernels, sublayer(): pl.pallas_call(sublayer_kernel, out_shape=tuple([jax.ShapeDtypeStruct(blo...  145 us
    pallas_call x1, Pallas kernels, hand_over(): pl.pallas_call(hand_over_kernel, out_shape=tuple((jax.ShapeDtypeStruct(a....  4.22 us

profile of v2, /device:TPU:41, one launch (start us, length us, event | category | flops | bytes accessed | tf_op | source)
XLA Modules:
  0.0 153.0 jit_solution(14269056421465977665)
XLA Ops:
  0.6 1.3 reshape.14.ids_ref
  1.9 1.5 broadcast_in_dim.2.ids_col
  3.4 145.3 %sublayer.1 = (bf16[512,384]{1,0:T(8,128)(2,1)}, bf16[512,384]{1,0:T(8,128)(2,1)}, bf16[512,384]{1,0:T(8,128)(2,1)}, bf16[512,384]{1,0:T(8,128)(2,1)}, bf16[384,3072]{1,0:T(8,128)(2,1)}) custom-call(s32[2,256]{1,0:T(2,128)} %reshape.14.ids_ref, s32[512,128]{1,0:T(8,128)} %broadcast_in_dim.2.ids_col, bf16[512,384]{1,0:T(8,128)(2,1)} %q_ref.1, ...), custom_call_target="tpu_custom_call" | custom-call | tf_op jit(solution)/shard_map/sublayer/pallas_call | solution.py:483
  148.8 4.2 %hand_over.1 = (bf16[512,384]{1,0:T(8,128)(2,1)}, bf16[512,384]{1,0:T(8,128)(2,1)}, bf16[512,384]{1,0:T(8,128)(2,1)}, bf16[512,384]{1,0:T(8,128)(2,1)}, bf16[384,3072]{1,0:T(8,128)(2,1)}) custom-call(bf16[512,384]{1,0:T(8,128)(2,1)} %get-tuple-element.10.refs_0_, bf16[512,384]{1,0:T(8,128)(2,1)} %get-tuple-element.11.refs_1_, ...), custom_call_target="tpu_custom_call" | custom-call | tf_op jit(solution)/shard_map/hand_over/pallas_call | solution.py:536

commit v3 on v2

v3 whole, which is shorter than its diff:
```python
import functools

import jax
import jax.numpy as jnp
from jax import lax
from jax.experimental import pallas as pl
from jax.experimental.pallas import tpu as pltpu
from jax.sharding import PartitionSpec as P

HEAD = 128
ROWS = 512
COLS = 384
HEADS_DEV = COLS // HEAD
TP = 8
FEATURES = TP * COLS
WINDOW = 5
OWN = 2
CHUNK = 256
HALF = ROWS // 2
PIECE_ROWS = 16
PIECE_COLS = 768
NEG = -1e30
SCALE = HEAD ** -0.5
EXP2_SCALE = SCALE * 1.4426950408889634
F32 = jnp.float32
BF16 = jnp.bfloat16
MESH = pl.DeviceIdType.MESH
VMEM = pl.BlockSpec(memory_space=pltpu.VMEM)
ANY = pl.BlockSpec(memory_space=pl.ANY)
LIMIT = 60 * 1024 * 1024


class Links:
    def __init__(self, send_sem, recv_sem):
        self.send_sem, self.recv_sem = send_sem, recv_sem
        self.sent = []

    def _copy(self, src, dst, role, where):
        return pltpu.make_async_remote_copy(
            src_ref=src,
            dst_ref=dst,
            send_sem=self.send_sem.at[role],
            recv_sem=self.recv_sem.at[role],
            device_id=where,
            device_id_type=MESH,
        )

    def send(self, src, dst, role, where, keep=True):
        copy = self._copy(src, dst, role, where)
        copy.start()
        if keep:
            self.sent.append(copy)

    def arrive(self, dst, role, where):
        self._copy(dst, dst, role, where).wait_recv()

    def left(self, src, role, where):
        self._copy(src, src, role, where).wait_send()

    def finish(self):
        for copy in self.sent:
            copy.wait_send()


def greet(peers):
    barrier = pltpu.get_barrier_semaphore()
    for where in peers:
        pl.semaphore_signal(barrier, inc=1, device_id=where, device_id_type=MESH)
    pl.semaphore_wait(barrier, len(peers))


def ctx_ring(place, step):
    return {"ctx": lax.rem(place + step + 32, 32)}


def columns(index):
    return pl.ds(pl.multiple_of(index * COLS, COLS), COLS)


IDS, KV, COT, DKV, MIX, FAR, SUM, ROLES = 0, 4, 16, 28, 40, 52, 53, 116
CORE, XR, ZR, ZG, XG, CG, SUM_ROLES = 0, 1, 7, 10, 13, 17, 21


def dot(a, b, contract):
    return lax.dot_general(
        a, b, ((contract[:1], contract[1:]), ((), ())), preferred_element_type=F32
    )


def wide(x, times):
    return jnp.concatenate([x] * times, axis=1)


def head_columns(h):
    return pl.ds(pl.multiple_of(h * HEAD, HEAD), HEAD)


def sublayer_kernel(
    ids_ref, q_ref, k_ref, v_ref, cot_ref, w_ref,
    mixed_ref, gq_ref, gk_ref, gv_ref, gw_ref,
    ids_all, ids_col, kv_all, cot_all, d_att, d_acc,
    top_ref, total_ref, out_acc, lse_ref, delta_ref, dq_acc, att, att_t,
    dkv, own, dkv_in,
    m_ref, m_hop, m_in, m_out, m_far,
    w_part, w_core, w_sum, w_hop, w_in, w_x, w_z,
    send_sem, recv_sem,
):
    place = lax.axis_index("ctx")
    part = lax.axis_index("tp")
    core = lax.rem(place, 2)
    z = lax.rem(lax.div(place, 2), 4)
    x = lax.div(place, 8)
    high = lax.rem(part, 2)
    flip = 1 - 2 * high
    after, before = ctx_ring(place, 2), ctx_ring(place, -2)
    sibling = {"ctx": place + 1 - 2 * core}
    x_up, x_down = ctx_ring(place, 8), ctx_ring(place, -8)
    z_to = [{"ctx": 8 * x + 2 * lax.rem(z + d, 4) + core} for d in (1, 2, 3)]
    z_from = [{"ctx": 8 * x + 2 * lax.rem(z + 4 - d, 4) + core} for d in (1, 2, 3)]
    up, down = lax.rem(part + 2, TP), lax.rem(part + 6, TP)
    across = lax.rem(part + 4, TP)
    over = part + flip
    y_up, y_down, far = {"tp": up}, {"tp": down}, {"tp": over}
    low, top = pl.ds(0, HALF), pl.ds(HALF, HALF)
    z_low, z_top = pl.ds(0, 2), pl.ds(2, 2)
    sib_slot, relay_slot = 3 - 2 * core, 1 + 2 * core
    direct_slot, sum_slot = 4 * core, 4 - 4 * core
    direct_to = {"ctx": lax.rem(place + 30 + 4 * core, 32)}
    sum_to = {"ctx": lax.rem(place + 34 - 4 * core, 32)}

    kv_all[OWN, 0] = k_ref[...]
    kv_all[OWN, 1] = v_ref[...]
    ids_all[OWN] = ids_ref[...].reshape(1, ROWS)
    greet([after, before, sibling, x_up, x_down, y_up, y_down, far] + z_to)
    links = Links(send_sem, recv_sem)

    links.send(cot_ref.at[low], cot_all.at[part, low], COT, far)
    links.send(cot_ref.at[top], cot_all.at[part, top], COT + 9, far)
    links.send(cot_ref, cot_all.at[part], COT + 1, y_up)
    links.send(cot_ref, cot_all.at[part], COT + 2, y_down)
    links.send(ids_all.at[OWN], ids_all.at[0], IDS, after)
    links.send(ids_all.at[OWN], ids_all.at[4], IDS + 1, before)
    links.send(ids_all.at[OWN], ids_all.at[relay_slot], IDS + 2, sibling)

    def send_heads(h):
        mine = kv_all.at[OWN, :, :, head_columns(h)]
        role = KV + 4 * h
        links.send(mine, kv_all.at[0, :, :, head_columns(h)], role, after, False)
        links.send(mine, kv_all.at[4, :, :, head_columns(h)], role + 1, before, False)
        links.send(mine, kv_all.at[relay_slot, :, :, head_columns(h)], role + 2, sibling, False)

    send_heads(0)
    for n in range(ROWS // 128):
        piece = jnp.broadcast_to(ids_all[OWN, :, pl.ds(n * 128, 128)], (128, 128))
        ids_col[pl.ds(n * 128, 128), :] = jnp.transpose(piece)
    cot_all[part] = cot_ref[...]

    def project(block, first=False):
        term = dot(cot_all[block], w_ref[:, columns(block)], (1, 1))
        if first:
            d_acc[...] = term
        else:
            d_acc[...] += term

    def key_ids(slot):
        return ids_all[slot]

    def scores(h, slot):
        cols = head_columns(h)
        s = dot(q_ref[:, cols], kv_all[slot, 0, :, cols], (1, 1)) * EXP2_SCALE
        return jnp.where(wide(ids_col[...], ROWS // 128) == key_ids(slot), s, NEG)

    def lanes(op, s):
        return functools.reduce(op, [s[:, n : n + 128] for n in range(0, ROWS, 128)])

    def attend(h, slot, first=False):
        s = scores(h, slot)
        peak = jnp.max(lanes(jnp.maximum, s), axis=1, keepdims=True)
        peak = jnp.broadcast_to(peak, (ROWS, 128))
        if not first:
            old = top_ref[h]
            peak = jnp.maximum(old, peak)
            fade = jnp.exp2(old - peak)
        p = jnp.exp2(s - wide(peak, ROWS // 128))
        part_total = lanes(jnp.add, p)
        term = dot(p.astype(BF16), kv_all[slot, 1, :, head_columns(h)], (1, 0))
        if not first:
            part_total += total_ref[h] * fade
            term += out_acc[h] * fade
        total_ref[h] = part_total
        out_acc[h] = term
        top_ref[h] = peak

    def settle(h):
        cols = head_columns(h)
        total = jnp.sum(total_ref[h], axis=1, keepdims=True)
        attended = out_acc[h] * (1.0 / total)
        att_t[cols, :] = jnp.transpose(attended).astype(BF16)
        attended = attended.astype(BF16)
        att[:, cols] = attended
        lse_ref[...] = top_ref[h] + jnp.broadcast_to(jnp.log2(total), (ROWS, 128))
        delta = jnp.sum(
            attended.astype(F32) * d_att[:, cols].astype(F32), axis=1, keepdims=True
        )
        delta_ref[...] = jnp.broadcast_to(delta, (ROWS, 128))

    def back(h, slot, first=False, last=False):
        cols = head_columns(h)
        q, g = q_ref[:, cols], d_att[:, cols]
        k, v = kv_all[slot, 0, :, cols], kv_all[slot, 1, :, cols]
        weight = jnp.exp2(scores(h, slot) - wide(lse_ref[...], ROWS // 128))
        dots = dot(g, v, (1, 1))
        dscores = (weight * (dots - wide(delta_ref[...], ROWS // 128))).astype(BF16)
        dk = dot(dscores, q, (0, 0)) * SCALE
        dv = dot(weight.astype(BF16), g, (0, 0))
        dq = dot(dscores, k, (1, 0))
        if not first:
            dq += dq_acc[...]
        if last:
            own[0, :, cols] = dk
            own[1, :, cols] = dv
            gq_ref[:, cols] = (dq * SCALE).astype(BF16)
        else:
            dkv[slot, 0, :, cols] = dk.astype(BF16)
            dkv[slot, 1, :, cols] = dv.astype(BF16)
            dq_acc[...] = dq

    def each_head(work):
        def step(h, carry):
            work(h)
            return carry

        lax.fori_loop(0, HEADS_DEV, step, 0)

    def send_half(block, half, role, where):
        links.send(cot_all.at[block, half], cot_all.at[block, half], role, where, False)

    def halves(block, role):
        links.arrive(cot_all.at[block, low], role, y_down)
        links.arrive(cot_all.at[block, top], role + 1, y_up)

    project(part, first=True)
    each_head(lambda h: attend(h, OWN, first=True))
    links.arrive(cot_all.at[down], COT + 1, y_down)
    send_half(down, low, COT + 3, y_up)
    links.arrive(cot_all.at[up], COT + 2, y_up)
    send_half(up, top, COT + 4, y_down)
    send_heads(1)
    project(down)
    project(up)
    links.arrive(ids_all.at[0], IDS, before)
    links.arrive(ids_all.at[4], IDS + 1, after)
    links.send(ids_all.at[sum_slot], ids_all.at[sib_slot], IDS + 3, sibling)
    links.arrive(cot_all.at[over, low], COT, far)
    send_half(over, low, COT + 5, y_up)
    send_half(over, low, COT + 6, y_down)
    links.arrive(cot_all.at[over, top], COT + 9, far)
    send_half(over, top, COT + 10, y_up)
    send_half(over, top, COT + 11, y_down)
    project(over)
    send_heads(2)
    links.arrive(ids_all.at[sib_slot], IDS + 2, sibling)

    def attend_sibling(h):
        links.arrive(kv_all.at[sib_slot, :, :, head_columns(h)], KV + 4 * h + 2, sibling)
        attend(h, sib_slot)

    each_head(attend_sibling)
    halves(across, COT + 3)
    project(across)
    links.arrive(ids_all.at[relay_slot], IDS + 3, sibling)

    down_over, up_over, across_over = down + flip, up + flip, across + flip
    links.arrive(cot_all.at[down_over, low], COT + 5, y_down)
    send_half(down_over, low, COT + 7, y_up)
    links.arrive(cot_all.at[up_over, top], COT + 11, y_up)
    send_half(up_over, top, COT + 8, y_down)

    def rest_of_cotangent():
        links.arrive(cot_all.at[down_over, top], COT + 10, y_down)
        links.arrive(cot_all.at[up_over, low], COT + 6, y_up)
        project(down_over)
        project(up_over)
        halves(across_over, COT + 7)
        project(across_over)
        d_att[...] = d_acc[...].astype(BF16)

    planes = (0, flip)

    def share_plane(n):
        add = planes[n]
        role = MIX + 6 * n

        def mix(block):
            m_ref[block] = dot(att[...], w_ref[:, columns(block)], (1, 0)).astype(BF16)

        mix(across + add)
        links.send(m_ref.at[across + add, low], m_hop.at[n, 0], role, y_up, False)
        links.send(m_ref.at[across + add, top], m_hop.at[n, 1], role + 1, y_down, False)
        mix(up + add)
        links.send(m_ref.at[up + add, top], m_in.at[n, 0, top], role + 2, y_up, False)
        mix(down + add)
        links.send(m_ref.at[down + add, low], m_in.at[n, 1, low], role + 3, y_down, False)
        mix(part + add)

    def plane_hops(n):
        add = planes[n]
        role = MIX + 6 * n
        links.arrive(m_hop.at[n, 0], role, y_down)
        m_out[n, 0] = add_up(m_ref[up + add, low], m_hop[n, 0])
        links.send(m_out.at[n, 0], m_in.at[n, 0, low], role + 4, y_up, False)
        links.arrive(m_hop.at[n, 1], role + 1, y_up)
        m_out[n, 1] = add_up(m_ref[down + add, top], m_hop[n, 1])
        links.send(m_out.at[n, 1], m_in.at[n, 1, top], role + 5, y_down, False)

    def quarter(step):
        return lax.rem(x + step, 4)

    below, above, opposite = quarter(3), quarter(1), quarter(2)

    def weight_rows(h):
        rows = head_columns(h)

        def two_blocks(n, carry):
            for side in range(2):
                term = dot(att_t[rows, :], cot_all[2 * n + side], (1, 0)).astype(BF16)
                side_cols = pl.ds(side * COLS, COLS)
                for c in range(2):
                    for j in range(4):
                        first = (4 * c + j) * PIECE_ROWS
                        w_part[h, c, n, j, :, side_cols] = term[first : first + PIECE_ROWS]
            return carry

        lax.fori_loop(0, 4, two_blocks, 0)
        links.send(
            w_part.at[h, 1 - core], w_core.at[h], SUM + SUM_ROLES * h + CORE, sibling, False
        )

    def out_rows(h, c, first, count):
        start = h * HEAD + c * (HEAD // 2) + first * PIECE_ROWS
        return pl.ds(pl.multiple_of(start, PIECE_ROWS), count * PIECE_ROWS)

    def out_cols(block):
        return pl.ds(pl.multiple_of(block * PIECE_COLS, PIECE_COLS), PIECE_COLS)

    def add_up(*terms):
        return sum(t.astype(F32) for t in terms).astype(BF16)

    def sum_cores(h):
        role = SUM + SUM_ROLES * h
        links.arrive(w_core.at[h], role + CORE, sibling)

        def add(i, carry):
            w_sum[h, i] = add_up(w_part[h, core, i], w_core[h, i])
            return carry

        lax.fori_loop(0, 4, add, 0)
        role += XR
        links.send(w_sum.at[h, opposite, z_low], w_hop.at[h, 0], role, x_up, False)
        links.send(w_sum.at[h, opposite, z_top], w_hop.at[h, 1], role + 1, x_down, False)
        links.send(w_sum.at[h, above, z_top], w_in.at[h, 0, z_top], role + 2, x_up, False)
        links.send(w_sum.at[h, below, z_low], w_in.at[h, 1, z_low], role + 3, x_down, False)

    def sum_hops(h):
        role = SUM + SUM_ROLES * h + XR
        links.arrive(w_hop.at[h, 0], role, x_down)
        w_hop[h, 0] = add_up(w_sum[h, above, z_low], w_hop[h, 0])
        links.send(w_hop.at[h, 0], w_in.at[h, 0, z_low], role + 4, x_up, False)
        links.arrive(w_hop.at[h, 1], role + 1, x_up)
        w_hop[h, 1] = add_up(w_sum[h, below, z_top], w_hop[h, 1])
        links.send(w_hop.at[h, 1], w_in.at[h, 1, z_top], role + 5, x_down, False)

    def sum_x(h):
        role = SUM + SUM_ROLES * h + XR
        links.arrive(w_in.at[h, 0, z_top], role + 2, x_down)
        links.arrive(w_in.at[h, 1, z_low], role + 3, x_up)
        links.arrive(w_in.at[h, 0, z_low], role + 4, x_down)
        links.arrive(w_in.at[h, 1, z_top], role + 5, x_up)
        w_x[h] = add_up(w_sum[h, x], w_in[h, 0], w_in[h, 1])
        role = SUM + SUM_ROLES * h + ZR
        for d in range(3):
            links.send(w_x.at[h, lax.rem(z + d + 1, 4)], w_z.at[h, d], role + d, z_to[d], False)

    def sum_z(h):
        role = SUM + SUM_ROLES * h + ZR
        for d in range(3):
            links.arrive(w_z.at[h, d], role + d, z_from[d])
        mine = gw_ref.at[out_rows(h, core, z, 1), out_cols(x)]
        mine[...] = add_up(w_x[h, z], w_z[h, 0], w_z[h, 1], w_z[h, 2])
        role = SUM + SUM_ROLES * h + ZG
        for d in range(3):
            links.send(mine, mine, role + d, z_to[d], False)

    def spread_x(h):
        role = SUM + SUM_ROLES * h
        for d in range(3):
            rows = out_rows(h, core, lax.rem(z + 3 - d, 4), 1)
            links.arrive(gw_ref.at[rows, out_cols(x)], role + ZG + d, z_from[d])
        mine = gw_ref.at[out_rows(h, core, 0, 4), out_cols(x)]
        links.send(mine, mine, role + XG, x_up, False)
        links.send(mine, mine, role + XG + 1, x_down, False)
        links.send(mine, mine, role + CG, sibling, False)

    def spread_on(h):
        role = SUM + SUM_ROLES * h
        for n, (block, back_from, on_to) in enumerate(((below, x_down, x_up), (above, x_up, x_down))):
            whole = gw_ref.at[out_rows(h, core, 0, 4), out_cols(block)]
            part_of = gw_ref.at[out_rows(h, core, 2 * n, 2), out_cols(block)]
            links.arrive(whole, role + XG + n, back_from)
            links.send(part_of, part_of, role + XG + 2 + n, on_to, False)
            links.send(whole, whole, role + CG + 1 + n, sibling, False)

    def spread_cores(h):
        role = SUM + SUM_ROLES * h
        for n, back_from in enumerate((x_down, x_up)):
            part_of = gw_ref.at[out_rows(h, core, 2 * n, 2), out_cols(opposite)]
            links.arrive(part_of, role + XG + 2 + n, back_from)
        whole = gw_ref.at[out_rows(h, core, 0, 4), out_cols(opposite)]
        links.send(whole, whole, role + CG + 3, sibling, False)

    def spread_done(h):
        role = SUM + SUM_ROLES * h + CG
        for n, block in enumerate((x, below, above, opposite)):
            links.arrive(gw_ref.at[out_rows(h, 1 - core, 0, 4), out_cols(block)], role + n, sibling)

    def sum_left(h):
        role = SUM + SUM_ROLES * h
        links.left(w_core.at[h], role + CORE, sibling)
        for n in range(6):
            links.left(w_hop.at[h, 0], role + XR + n, x_up)
        for n in range(3):
            links.left(w_z.at[h, n], role + ZR + n, z_to[n])
            links.left(w_z.at[h, n], role + ZG + n, z_to[n])
        whole = gw_ref.at[out_rows(h, core, 0, 4), out_cols(x)]
        half = gw_ref.at[out_rows(h, core, 0, 2), out_cols(x)]
        for n in range(2):
            links.left(whole, role + XG + n, x_up)
            links.left(half, role + XG + 2 + n, x_up)
        for n in range(4):
            links.left(whole, role + CG + n, sibling)

    final = HEADS_DEV - 1

    def per_head(h):
        def of_last(step):
            pl.when(h > 0)(lambda: step(h - 1))

        cols = head_columns(h)
        role = KV + 4 * h
        links.arrive(kv_all.at[0, :, :, cols], role, before)
        links.arrive(kv_all.at[4, :, :, cols], role + 1, after)
        links.send(
            kv_all.at[sum_slot, :, :, cols], kv_all.at[sib_slot, :, :, cols], role + 3, sibling,
            False,
        )
        attend(h, 0)
        attend(h, 4)
        pl.when(h == 0)(rest_of_cotangent)
        links.arrive(kv_all.at[relay_slot, :, :, cols], role + 3, sibling)
        attend(h, relay_slot)
        settle(h)
        pl.when(h == final)(lambda: share_plane(1))
        weight_rows(h)
        role = DKV + 4 * h
        back(h, relay_slot, first=True)
        links.send(
            dkv.at[relay_slot, :, :, cols], dkv_in.at[1, :, :, cols], role + 1, sibling, False
        )
        sum_cores(h)
        back(h, direct_slot)
        links.send(
            dkv.at[direct_slot, :, :, cols], dkv_in.at[2 + core, :, :, cols], role + 2 + core,
            direct_to, False,
        )
        of_last(sum_x)
        back(h, sum_slot)
        links.arrive(dkv_in.at[1, :, :, cols], role + 1, sibling)
        for n in range(2):
            dkv[sum_slot, n, :, cols] = add_up(
                dkv[sum_slot, n, :, cols], dkv_in[1, n, :, cols]
            )
        links.send(
            dkv.at[sum_slot, :, :, cols], dkv_in.at[3 - core, :, :, cols], role + 3 - core,
            sum_to, False,
        )
        back(h, sib_slot)
        links.send(dkv.at[sib_slot, :, :, cols], dkv_in.at[0, :, :, cols], role, sibling, False)

        @pl.when(h == final)
        def _():
            plane_hops(1)
            share_plane(0)

        sum_hops(h)
        back(h, OWN, last=True)

    each_head(per_head)

    def along_y(n):
        add = planes[n]
        role = MIX + 6 * n
        links.arrive(m_in.at[n, 0, top], role + 2, y_down)
        links.arrive(m_in.at[n, 1, low], role + 3, y_up)
        links.arrive(m_in.at[n, 0, low], role + 4, y_down)
        links.arrive(m_in.at[n, 1, top], role + 5, y_up)
        return add_up(m_ref[part + add], m_in[n, 0], m_in[n, 1])

    def add_keys(h):
        cols = head_columns(h)
        role = DKV + 4 * h
        links.arrive(dkv_in.at[0, :, :, cols], role, sibling)
        links.arrive(dkv_in.at[2, :, :, cols], role + 2, after)
        links.arrive(dkv_in.at[3, :, :, cols], role + 3, before)
        for n, out in enumerate((gk_ref, gv_ref)):
            out[:, cols] = add_up(
                own[n, :, cols], dkv_in[0, n, :, cols], dkv_in[2, n, :, cols],
                dkv_in[3, n, :, cols],
            )

    sum_x(final)
    sum_z(0)
    sum_z(1)
    plane_hops(0)
    spread_x(0)
    spread_x(1)
    sum_z(final)
    m_far[0] = along_y(1)
    links.send(m_far.at[0], m_far.at[1], FAR, far)
    spread_on(0)
    spread_on(1)
    spread_x(final)
    spread_cores(0)
    spread_cores(1)
    m_in[0, 0] = along_y(0)
    spread_on(final)
    each_head(add_keys)
    spread_cores(final)
    links.arrive(m_far.at[1], FAR, far)
    mixed_ref[...] = add_up(m_in[0, 0], m_far[1])
    each_head(spread_done)

    def heads_left(h):
        cols = head_columns(h)
        for n in range(4):
            links.left(kv_all.at[OWN, :, :, cols], KV + 4 * h + n, sibling)
            links.left(dkv.at[OWN, :, :, cols], DKV + 4 * h + n, sibling)
        sum_left(h)

    each_head(heads_left)
    for n in range(2):
        for k in range(6):
            links.left(m_hop.at[n, 0], MIX + 6 * n + k, y_up)
    for role in (3, 4, 5, 6, 7, 8, 10, 11):
        links.left(cot_all.at[0, low], COT + role, y_up)
    links.finish()


def sublayer(ids, query, keys, values, cotangent, weight):
    block = (ROWS, COLS)
    bf16 = lambda *shape: pltpu.VMEM(shape, BF16)
    f32 = lambda *shape: pltpu.VMEM(shape, F32)
    heads = (HEADS_DEV, ROWS, HEAD)
    piece = (PIECE_ROWS, PIECE_COLS)
    return pl.pallas_call(
        sublayer_kernel,
        out_shape=tuple([jax.ShapeDtypeStruct(block, BF16)] * 4)
        + (jax.ShapeDtypeStruct((COLS, FEATURES), BF16),),
        in_specs=[VMEM] * 6,
        out_specs=(VMEM,) * 5,
        scratch_shapes=[
            pltpu.VMEM((WINDOW, 1, ROWS), jnp.int32),
            pltpu.VMEM((ROWS, 128), jnp.int32),
            bf16(WINDOW, 2, *block),
            bf16(TP, *block),
            bf16(*block),
            f32(*block),
            f32(*heads),
            f32(*heads),
            f32(*heads),
            f32(ROWS, HEAD),
            f32(ROWS, HEAD),
            f32(ROWS, HEAD),
            bf16(*block),
            bf16(COLS, ROWS),
            bf16(WINDOW, 2, *block),
            f32(2, *block),
            bf16(4, 2, *block),
            bf16(TP, *block),
            bf16(2, 2, HALF, COLS),
            bf16(2, 2, *block),
            bf16(2, 2, HALF, COLS),
            bf16(2, *block),
            bf16(HEADS_DEV, 2, 4, 4, *piece),
            bf16(HEADS_DEV, 4, 4, *piece),
            bf16(HEADS_DEV, 4, 4, *piece),
            bf16(HEADS_DEV, 2, 2, *piece),
            bf16(HEADS_DEV, 2, 4, *piece),
            bf16(HEADS_DEV, 4, *piece),
            bf16(HEADS_DEV, 3, *piece),
            pltpu.SemaphoreType.DMA((ROLES,)),
            pltpu.SemaphoreType.DMA((ROLES,)),
        ],
        compiler_params=pltpu.CompilerParams(
            collective_id=0, has_side_effects=True, vmem_limit_bytes=LIMIT
        ),
        name="sublayer",
    )(ids, query, keys, values, cotangent, weight)


def hand_over_kernel(*refs):
    count = len(refs) // 2
    for n in range(count):
        refs[count + n][...] = refs[n][...]


def hand_over(arrays):
    return pl.pallas_call(
        hand_over_kernel,
        out_shape=tuple(jax.ShapeDtypeStruct(a.shape, a.dtype) for a in arrays),
        in_specs=[VMEM] * len(arrays),
        out_specs=(VMEM,) * len(arrays),
        name="hand_over",
    )(*arrays)


def on_device(query, keys, values, image_ids, out_weight, cotangent):
    return hand_over(sublayer(image_ids, query, keys, values, cotangent, out_weight))


def solution(mesh):
    placed = (
        P("ctx", "tp"),
        P("ctx", "tp"),
        P("ctx", "tp"),
        P("ctx"),
        P("tp", None),
        P("ctx", "tp"),
    )
    return jax.shard_map(
        on_device,
        mesh=mesh,
        in_specs=placed,
        out_specs=(P("ctx", "tp"), P("ctx", "tp"), P("ctx", "tp"), P("ctx", "tp"), P("tp", None)),
        check_vma=False,
    )
```

time: 154 us -> 143 us (0.929)
  the two profiles are of different devices: /device:TPU:41 before, /device:TPU:105 now
where the time goes in v3:
time: 143 us
  Pallas kernels  143 us (100%)
    pallas_call x1, Pallas kernels, sublayer(): pl.pallas_call(sublayer_kernel, out_shape=tuple([jax.ShapeDtypeStruct(blo...  138 us
    pallas_call x1, Pallas kernels, hand_over(): pl.pallas_call(hand_over_kernel, out_shape=tuple((jax.ShapeDtypeStruct(a....  4.22 us

profile of v3, /device:TPU:105, one launch (start us, length us, event | category | flops | bytes accessed | tf_op | source)
XLA Modules:
  0.0 143.2 jit_solution(13380158601454223010)
XLA Ops:
  0.6 138.3 %sublayer.1 = (bf16[512,384]{1,0:T(8,128)(2,1)}, bf16[512,384]{1,0:T(8,128)(2,1)}, bf16[512,384]{1,0:T(8,128)(2,1)}, bf16[512,384]{1,0:T(8,128)(2,1)}, bf16[384,3072]{1,0:T(8,128)(2,1)}) custom-call(s32[512]{0:T(512)} %ids_ref.1, bf16[512,384]{1,0:T(8,128)(2,1)} %q_ref.1, bf16[512,384]{1,0:T(8,128)(2,1)} %k_ref.1, bf16[512,384]{1,0:T(8,128)(2,1)} %v_ref.1, ...), custom_call_target="tpu_custom_call" | custom-call | tf_op jit(solution)/shard_map/sublayer/pallas_call | solution.py:564
  139.0 4.2 %hand_over.1 = (bf16[512,384]{1,0:T(8,128)(2,1)}, bf16[512,384]{1,0:T(8,128)(2,1)}, bf16[512,384]{1,0:T(8,128)(2,1)}, bf16[512,384]{1,0:T(8,128)(2,1)}, bf16[384,3072]{1,0:T(8,128)(2,1)}) custom-call(bf16[512,384]{1,0:T(8,128)(2,1)} %get-tuple-element.10.refs_0_, bf16[512,384]{1,0:T(8,128)(2,1)} %get-tuple-element.11.refs_1_, ...), custom_call_target="tpu_custom_call" | custom-call | tf_op jit(solution)/shard_map/hand_over/pallas_call | solution.py:617

commit v4 on v3

--- a/solution.py
+++ b/solution.py
@@ -459,8 +459,8 @@
         links.arrive(kv_all.at[relay_slot, :, :, cols], role + 3, sibling)
         attend(h, relay_slot)
         settle(h)
+        weight_rows(h)
         pl.when(h == final)(lambda: share_plane(1))
-        weight_rows(h)
         role = DKV + 4 * h
         back(h, relay_slot, first=True)
         links.send(
@@ -472,7 +472,6 @@
             dkv.at[direct_slot, :, :, cols], dkv_in.at[2 + core, :, :, cols], role + 2 + core,
             direct_to, False,
         )
-        of_last(sum_x)
         back(h, sum_slot)
         links.arrive(dkv_in.at[1, :, :, cols], role + 1, sibling)
         for n in range(2):
@@ -483,16 +482,13 @@
             dkv.at[sum_slot, :, :, cols], dkv_in.at[3 - core, :, :, cols], role + 3 - core,
             sum_to, False,
         )
+        sum_hops(h)
         back(h, sib_slot)
         links.send(dkv.at[sib_slot, :, :, cols], dkv_in.at[0, :, :, cols], role, sibling, False)
-
-        @pl.when(h == final)
-        def _():
-            plane_hops(1)
-            share_plane(0)
-
-        sum_hops(h)
+        pl.when(h == final)(lambda: plane_hops(1))
         back(h, OWN, last=True)
+        sum_x(h)
+        of_last(sum_z)
 
     each_head(per_head)
 
@@ -517,18 +513,16 @@
                 dkv_in[3, n, :, cols],
             )
 
-    sum_x(final)
-    sum_z(0)
-    sum_z(1)
-    plane_hops(0)
+    share_plane(0)
+    sum_z(final)
     spread_x(0)
     spread_x(1)
-    sum_z(final)
-    m_far[0] = along_y(1)
-    links.send(m_far.at[0], m_far.at[1], FAR, far)
+    plane_hops(0)
     spread_on(0)
     spread_on(1)
     spread_x(final)
+    m_far[0] = along_y(1)
+    links.send(m_far.at[0], m_far.at[1], FAR, far)
     spread_cores(0)
     spread_cores(1)
     m_in[0, 0] = along_y(0)

time: 143 us -> 140 us (0.979)
  the two profiles are of different devices: /device:TPU:105 before, /device:TPU:2 now
where the time goes in v4:
time: 140 us
  Pallas kernels  139 us (99%)
    pallas_call x1, Pallas kernels, sublayer(): pl.pallas_call(sublayer_kernel, out_shape=tuple([jax.ShapeDtypeStruct(blo...  135 us
    pallas_call x1, Pallas kernels, hand_over(): pl.pallas_call(hand_over_kernel, out_shape=tuple((jax.ShapeDtypeStruct(a....  4.22 us

profile of v4, /device:TPU:2, one launch (start us, length us, event | category | flops | bytes accessed | tf_op | source)
XLA Modules:
  0.0 139.5 jit_solution(3322478060103267368)
XLA Ops:
  0.6 134.6 %sublayer.1 = (bf16[512,384]{1,0:T(8,128)(2,1)}, bf16[512,384]{1,0:T(8,128)(2,1)}, bf16[512,384]{1,0:T(8,128)(2,1)}, bf16[512,384]{1,0:T(8,128)(2,1)}, bf16[384,3072]{1,0:T(8,128)(2,1)}) custom-call(s32[512]{0:T(512)} %ids_ref.1, bf16[512,384]{1,0:T(8,128)(2,1)} %q_ref.1, bf16[512,384]{1,0:T(8,128)(2,1)} %k_ref.1, bf16[512,384]{1,0:T(8,128)(2,1)} %v_ref.1, ...), custom_call_target="tpu_custom_call" | custom-call | tf_op jit(solution)/shard_map/sublayer/pallas_call | solution.py:558
  135.3 4.2 %hand_over.1 = (bf16[512,384]{1,0:T(8,128)(2,1)}, bf16[512,384]{1,0:T(8,128)(2,1)}, bf16[512,384]{1,0:T(8,128)(2,1)}, bf16[512,384]{1,0:T(8,128)(2,1)}, bf16[384,3072]{1,0:T(8,128)(2,1)}) custom-call(bf16[512,384]{1,0:T(8,128)(2,1)} %get-tuple-element.10.refs_0_, bf16[512,384]{1,0:T(8,128)(2,1)} %get-tuple-element.11.refs_1_, ...), custom_call_target="tpu_custom_call" | custom-call | tf_op jit(solution)/shard_map/hand_over/pallas_call | solution.py:611

commit v5 on v4

--- a/solution.py
+++ b/solution.py
@@ -518,17 +518,17 @@
     spread_x(0)
     spread_x(1)
     plane_hops(0)
-    spread_on(0)
-    spread_on(1)
     spread_x(final)
     m_far[0] = along_y(1)
     links.send(m_far.at[0], m_far.at[1], FAR, far)
+    spread_on(0)
+    spread_on(1)
     spread_cores(0)
     spread_cores(1)
+    spread_on(final)
     m_in[0, 0] = along_y(0)
-    spread_on(final)
+    spread_cores(final)
     each_head(add_keys)
-    spread_cores(final)
     links.arrive(m_far.at[1], FAR, far)
     mixed_ref[...] = add_up(m_in[0, 0], m_far[1])
     each_head(spread_done)

time: 140 us -> 137 us (0.979)
  the two profiles are of different devices: /device:TPU:2 before, /device:TPU:38 now
where the time goes in v5:
time: 137 us
  Pallas kernels  136 us (99%)
    pallas_call x1, Pallas kernels, sublayer(): pl.pallas_call(sublayer_kernel, out_shape=tuple([jax.ShapeDtypeStruct(blo...  132 us
    pallas_call x1, Pallas kernels, hand_over(): pl.pallas_call(hand_over_kernel, out_shape=tuple((jax.ShapeDtypeStruct(a....  4.22 us

profile of v5, /device:TPU:38, one launch (start us, length us, event | category | flops | bytes accessed | tf_op | source)
XLA Modules:
  0.0 137.0 jit_solution(10076396042406238957)
XLA Ops:
  0.6 132.1 %sublayer.1 = (bf16[512,384]{1,0:T(8,128)(2,1)}, bf16[512,384]{1,0:T(8,128)(2,1)}, bf16[512,384]{1,0:T(8,128)(2,1)}, bf16[512,384]{1,0:T(8,128)(2,1)}, bf16[384,3072]{1,0:T(8,128)(2,1)}) custom-call(s32[512]{0:T(512)} %ids_ref.1, bf16[512,384]{1,0:T(8,128)(2,1)} %q_ref.1, bf16[512,384]{1,0:T(8,128)(2,1)} %k_ref.1, bf16[512,384]{1,0:T(8,128)(2,1)} %v_ref.1, ...), custom_call_target="tpu_custom_call" | custom-call | tf_op jit(solution)/shard_map/sublayer/pallas_call | solution.py:558
  132.8 4.2 %hand_over.1 = (bf16[512,384]{1,0:T(8,128)(2,1)}, bf16[512,384]{1,0:T(8,128)(2,1)}, bf16[512,384]{1,0:T(8,128)(2,1)}, bf16[512,384]{1,0:T(8,128)(2,1)}, bf16[384,3072]{1,0:T(8,128)(2,1)}) custom-call(bf16[512,384]{1,0:T(8,128)(2,1)} %get-tuple-element.10.refs_0_, bf16[512,384]{1,0:T(8,128)(2,1)} %get-tuple-element.11.refs_1_, ...), custom_call_target="tpu_custom_call" | custom-call | tf_op jit(solution)/shard_map/hand_over/pallas_call | solution.py:611
